TPU v7x, 256 devices: a whole 4x4x8 slice. The times are simulated.
256 devices in a mesh: seq: 16 (over x_lo, y, core), head: 16 (over x_hi, z).
Axes of the slice: x: 4 (x_hi: 2, x_lo: 2; x = x_hi * 2 + x_lo), y: 4, z: 8, core: 2. Of those that a mesh axis runs over, the one named last changes fastest.
Arguments:
- tokens: bfloat16 [3072, 8192], P('seq', 'head'), may hold values from -6 to 6
- query_weight: bfloat16 [8192, 8192], P(None, 'head'), may hold values from -4 to 4
- kv_weight: bfloat16 [8192, 2048], P(None, 'head'), may hold values from -1 to 1
- signs: int32 [456, 8192], P(None, 'head'), may hold values from 0 to 262143, as said below
- cotangent: bfloat16 [3072, 8192], P('seq', 'head'), may hold values from -0.109375 to 0.109375
Outputs:
- salience: float32 [8192, 8192], P('seq', 'head')
Inputs may be any that keep to these rules, and one draw needn't show every extreme that they name: `signs`: bit b of word w gives the sign of query weight row 18 w + b; bits for rows at or past 8192 are not used.
All inputs are finite; a program needn't handle non-finite values.
Results may differ from a plain program's by a relative error of at most 0.012.
The roundings to bfloat16 on the way count: a program that leaves them out, or rounds other values in their place, can miss the bound.
Values may be sent and summed in bfloat16 or wider, within the bound.
A program may use at most 128 MiB of HBM per device.

v0:
```python
import jax
import jax.numpy as jnp
from jax import lax
from jax.sharding import PartitionSpec as P


def swapped(block, axis, stride):
    count = lax.axis_size(axis)
    route = []
    for low in range(count):
        high = low | 1 << stride
        if high != low and high < count:
            route += [(low, high), (high, low)]
    return lax.ppermute(block, axis, route)


def folded(share, axis, dim, lap, start):

    def gathered(part):
        return lax.all_gather(part, axis, axis=dim, tiled=True)

    return lap(start, jax.tree.map(gathered, share), jnp.int32(0))


def decode_rows(packed, row_count):
    shifts = jnp.arange(18, dtype=jnp.int32)
    bits = packed[:, None, :] >> shifts[None, :, None] & 1
    bits = bits.reshape(-1, packed.shape[1])[:row_count]
    return (2 * bits - 1).astype(jnp.float32)


def over_blocks(step_fn, carry, key_piece, value_piece):
    piece_rows = key_piece.shape[0]
    block_count = piece_rows // 1024
    block_rows = piece_rows // block_count

    def one_turn(turn_index, running):
        key_block = lax.dynamic_slice_in_dim(key_piece, turn_index * block_rows, block_rows, 0)
        value_block = lax.dynamic_slice_in_dim(value_piece, turn_index * block_rows, block_rows, 0)
        return step_fn(running, key_block, value_block, turn_index * block_rows)

    return lax.fori_loop(0, block_count, one_turn, carry)


def local(tokens, query_weight, kv_weight, signs, cotangent):
    head_size = kv_weight.shape[1]
    half_width = head_size // 2
    local_heads = query_weight.shape[1] // head_size
    local_tokens = tokens.shape[0]
    score_scale = head_size ** (-0.5)
    full_tokens = lax.all_gather(tokens, "head", axis=1, tiled=True)
    model_width = full_tokens.shape[1]
    sign_full = decode_rows(signs, model_width)
    query_local = jnp.dot(full_tokens, query_weight, preferred_element_type=jnp.float32).astype(
        jnp.bfloat16
    )
    tangent_local = jnp.dot(
        full_tokens, sign_full.astype(jnp.bfloat16), preferred_element_type=jnp.float32
    ).astype(jnp.bfloat16)
    own_part = jnp.dot(full_tokens, kv_weight, preferred_element_type=jnp.float32).astype(
        jnp.bfloat16
    )
    partner = swapped(own_part, "head", 0)
    odd_member = lax.axis_index("head") % 2 == 1
    lower_part = jnp.where(odd_member, partner, own_part)
    upper_part = jnp.where(odd_member, own_part, partner)
    key_local = jnp.concatenate([lower_part[:, :half_width], upper_part[:, :half_width]], axis=1)
    value_local = jnp.concatenate([lower_part[:, half_width:], upper_part[:, half_width:]], axis=1)

    def to_rows(matrix):
        return (
            matrix.reshape(local_tokens, local_heads, head_size)
            .transpose(1, 0, 2)
            .reshape(local_heads * local_tokens, head_size)
        )

    query_rows = to_rows(query_local)
    tangent_rows = to_rows(tangent_local)
    cot_rows = to_rows(cotangent)
    cot_float = cot_rows.astype(jnp.float32)
    row_count = query_rows.shape[0]
    query_pos = lax.axis_index("seq") * local_tokens + jnp.tile(
        jnp.arange(local_tokens, dtype=jnp.int32), local_heads
    )

    def scores(key_piece, start):
        key_pos = start + jnp.arange(key_piece.shape[0], dtype=jnp.int32)
        visible = key_pos[None, :] <= query_pos[:, None]
        logits = (
            jnp.einsum("rd,kd->rk", query_rows, key_piece, preferred_element_type=jnp.float32)
            * score_scale
        )
        logit_tangent = (
            jnp.einsum("rd,kd->rk", tangent_rows, key_piece, preferred_element_type=jnp.float32)
            * score_scale
        )
        return (jnp.where(visible, logits, -1e30), logit_tangent, visible)

    def first_step(carry, key_piece, value_piece, start):
        row_max, row_total, centre_sum = carry
        masked, logit_tangent, visible = scores(key_piece, start)
        new_max = jnp.maximum(row_max, jnp.max(masked, axis=1))
        shrink = jnp.exp(row_max - new_max)
        weights_exp = jnp.where(visible, jnp.exp(masked - new_max[:, None]), 0.0)
        return (
            new_max,
            row_total * shrink + jnp.sum(weights_exp, axis=1),
            centre_sum * shrink + jnp.sum(weights_exp * logit_tangent, axis=1),
        )

    start_stats = (
        jnp.full((row_count,), -1e30, jnp.float32),
        jnp.zeros((row_count,), jnp.float32),
        jnp.zeros((row_count,), jnp.float32),
    )
    stats = folded(
        key_local,
        "seq",
        0,
        lambda carry, piece, start: over_blocks(first_step, carry, piece, piece),
        start_stats,
    )
    row_max, row_total, centre_sum = stats
    centre = centre_sum / row_total

    def probabilities(key_piece, start):
        masked, logit_tangent, visible = scores(key_piece, start)
        probs = jnp.where(visible, jnp.exp(masked - row_max[:, None]) / row_total[:, None], 0.0)
        return (probs, probs * (logit_tangent - centre[:, None]))

    def second_step(carry, key_piece, value_piece, start):
        probs, probs_tangent = probabilities(key_piece, start)
        output_sum = carry[0] + jnp.dot(
            probs.astype(jnp.bfloat16), value_piece, preferred_element_type=jnp.float32
        )
        output_tangent = carry[1] + jnp.dot(
            probs_tangent.astype(jnp.bfloat16), value_piece, preferred_element_type=jnp.float32
        )
        return (output_sum, output_tangent)

    empty_rows = jnp.zeros((row_count, head_size), jnp.float32)
    outputs = folded(
        (key_local, value_local),
        "seq",
        0,
        lambda carry, pieces, start: over_blocks(second_step, carry, pieces[0], pieces[1]),
        (empty_rows, empty_rows),
    )
    delta = jnp.sum(cot_float * outputs[0], axis=1)
    delta_tangent = jnp.sum(cot_float * outputs[1], axis=1)

    def third_step(running, key_piece, value_piece, start):
        probs, probs_tangent = probabilities(key_piece, start)
        back = jnp.einsum("rd,kd->rk", cot_rows, value_piece, preferred_element_type=jnp.float32)
        score_tangent = probs_tangent * (back - delta[:, None]) - probs * delta_tangent[:, None]
        return running + jnp.dot(
            score_tangent.astype(jnp.bfloat16), key_piece, preferred_element_type=jnp.float32
        )

    update_sum = folded(
        (key_local, value_local),
        "seq",
        0,
        lambda carry, pieces, start: over_blocks(third_step, carry, pieces[0], pieces[1]),
        empty_rows,
    )
    update_rows = (update_sum * score_scale).astype(jnp.bfloat16)
    update_local = (
        update_rows.reshape(local_heads, local_tokens, head_size)
        .transpose(1, 0, 2)
        .reshape(local_tokens, local_heads * head_size)
    )
    owned_rows = model_width // lax.axis_size("seq")
    owned_start = lax.axis_index("seq") * owned_rows
    hessian = lax.psum_scatter(
        lax.dot_general(
            full_tokens, update_local, (((0,), (0,)), ((), ())), preferred_element_type=jnp.float32
        ),
        "seq",
        scatter_dimension=0,
        tiled=True,
    )
    owned_signs = lax.dynamic_slice_in_dim(sign_full, owned_start, owned_rows, 0)
    return owned_signs * hessian


def solution(mesh):
    placed = (P("seq", "head"), P(None, "head"), P(None, "head"), P(None, "head"), P("seq", "head"))
    return jax.shard_map(
        local, mesh=mesh, in_specs=placed, out_specs=P("seq", "head"), check_vma=False
    )
```

profile of v0, /device:TPU:1, one launch (start us, length us, event | category | flops | bytes accessed | tf_op | source)
XLA Modules:
  0.0 363.3 jit_solution(5157205453494968636)
XLA Ops:
  6.5 0.7 all-gather.2.cloned.1.call-update
  7.4 11.6 %shift_right_arithmetic.20 = s32[456,18,512]{2,1,0:T(8,128)} broadcast(s32[456,512]{1,0:T(8,128)} %param.14), dimensions={0,2} | broadcast | bytes 17743872 | tf_op jit(solution)/shard_map/shift_right_arithmetic | solution.py:27
  18.9 19.7 %shift_right_arithmetic.21 = s32[8208,512]{1,0:T(8,128)} reshape(s32[456,18,512]{2,1,0:T(8,128)} %shift_right_arithmetic.20) | data formatting | bytes 33619968 | tf_op jit(solution)/shard_map/shift_right_arithmetic | solution.py:27
  38.9 0.7 copy_bitcast_fusion
  39.6 12.1 %fusion.61 = f32[8192,512]{1,0:T(8,128)} fusion(s32[8208,512]{1,0:T(8,128)} %shift_right_arithmetic.21, s32[8192]{0:T(1024)S(1)} %slice.21), kind=kLoop, calls=%fused_computation.73 | loop fusion | flops 20971520 | bytes 33587200 | tf_op jit(solution)/shard_map/convert_element_type | solution.py:29
  51.8 53.9 %all-gather.2.cloned.1.call-done = bf16[192,8192]{1,0:T(8,128)(2,1)} async-done(((bf16[192,512]{1,0:T(8,128)(2,1)}), bf16[192,8192]{1,0:T(8,128)(2,1)}) %all-gather.2.cloned.1.call-update) | async-done | bytes 3145744 | tf_op jit(solution)/shard_map/all_gather | solution.py:51
  105.7 3.0 convolution_convert_fusion.1
  108.8 7.7 %fusion.67 = bf16[192,512]{1,0:T(8,128)(2,1)S(1)} fusion(bf16[192,8192]{1,0:T(8,128)(2,1)S(1)} %copy-done.2, f32[8192,512]{1,0:T(8,128)} %fusion.61), kind=kOutput, calls=%fused_computation.79 | convolution fusion | flops 1614905344 | bytes 20119552 | tf_op jit(solution)/shard_map/dot_general | solution.py:57
  116.6 1.8 convolution_convert_fusion
  118.6 0.7 fusion.74
  119.4 27.1 %all_gather.13 = bf16[3072,128]{1,0:T(8,128)(2,1)} all-gather(bf16[192,128]{1,0:T(8,128)(2,1)S(1)} %pad_maximum_fusion), channel_id=1, replica_groups=mesh['seq'=16,'head'=16] {'seq'}, dimensions={0}, use_global_device_ids=true | all-gather | bytes 835584 | tf_op jit(solution)/shard_map/all_gather | solution.py:20
  146.5 19.8 %while.48 = (s32[]{:T(128)}, f32[768]{0:T(1024)S(1)}, f32[768]{0:T(1024)S(1)}, f32[768]{0:T(1024)}, bf16[3072,128]{1,0:T(8,128)(2,1)}, /*index=5*/bf16[768,128]{...) while((s32[]{:T(128)}, f32[768]{0:T(1024)S(1)}, ...), condition=%wide.region_4.5_spmd.clone, body=%wide.region_0.4_spmd.clone.sunk | while | flops 416816128 | bytes 10469622 | solution.py:42
  146.6 2.1 fusion.119
  149.4 0.9 fusion.121
  150.3 2.1 fusion.120
  153.2 2.2 fusion.119
  156.0 0.9 fusion.121
  156.9 2.1 fusion.120
  159.8 2.1 fusion.119
  162.6 0.9 fusion.121
  163.5 2.1 fusion.120
  166.3 0.9 pad_maximum_fusion.1
  167.2 20.0 %all_gather.14 = bf16[3072,128]{1,0:T(8,128)(2,1)} all-gather(bf16[192,128]{1,0:T(8,128)(2,1)S(1)} %pad_maximum_fusion.1), channel_id=1, replica_groups=mesh['seq'=16,'head'=16] {'seq'}, dimensions={0}, use_global_device_ids=true | all-gather | bytes 835584 | tf_op jit(solution)/shard_map/all_gather | solution.py:20
  187.9 24.4 %while.49 = (s32[]{:T(128)}, f32[768,128]{1,0:T(8,128)}, f32[768,128]{1,0:T(8,128)}, bf16[3072,128]{1,0:T(8,128)(2,1)}, bf16[768,128]{1,0:T(8,128)(2,1)S(1)}, /*...) while((s32[]{:T(128)}, f32[768,128]{1,0:T(8,128)}, ...), condition=%wide.region_6.7_spmd.clone, body=%wide.region_5.6_spmd.clone.sunk | while | flops 814352128 | bytes 12484309 | solution.py:42
  188.5 2.0 compare_select_fusion.7
  190.5 3.0 fusion.131
  193.5 2.3 fusion.130
  196.5 2.0 compare_select_fusion.7
  198.5 3.1 fusion.131
  201.6 2.4 fusion.130
  204.7 2.0 compare_select_fusion.7
  206.7 3.1 fusion.131
  209.8 2.4 fusion.130
  212.3 2.1 fusion.71
  214.4 32.8 %while.50 = (s32[]{:T(128)}, f32[768,128]{1,0:T(8,128)}, bf16[3072,128]{1,0:T(8,128)(2,1)}, bf16[768,128]{1,0:T(8,128)(2,1)S(1)}, f32[768]{0:T(1024)S(1)}, /*ind...) while((s32[]{:T(128)}, f32[768,128]{1,0:T(8,128)}, ...), condition=%wide.region_10.11_spmd.clone, body=%wide.region_9.10_spmd.clone.sunk | while | flops 816514816 | bytes 15048420 | solution.py:42
  214.4 1.5 fusion.139
  215.9 3.2 fusion.140
  220.3 4.9 %fusion.141 = f32[768,128]{1,0:T(8,128)} fusion(f32[1024,768]{1,0:T(8,128)S(1)} %fusion.139, f32[1024,768]{1,0:T(8,128)} %fusion.140, bf16[768,128]{1,0:T(8,128)(2,1)} %get-tuple-element.1070, f32[768]{0:T(1024)} %get-tuple-element.1072, f32[768]{0:T(1024)} %get-tuple-element.1071, f32[768]{0:T(1024)S(1)} %get-tuple-element.1068, ...), kind=kOutput, calls=%fused_computation.54.clone.1 | convolution fusion | flops 413859840 | bytes 7825920 | tf_op jit(solution)/shard_map/while/body/eval_jaxpr/dot_general | solution.py:156
  225.2 1.5 fusion.139
  226.8 3.2 fusion.140
  231.2 5.0 %fusion.141 = f32[768,128]{1,0:T(8,128)} fusion(f32[1024,768]{1,0:T(8,128)S(1)} %fusion.139, f32[1024,768]{1,0:T(8,128)} %fusion.140, bf16[768,128]{1,0:T(8,128)(2,1)} %get-tuple-element.1070, f32[768]{0:T(1024)} %get-tuple-element.1072, f32[768]{0:T(1024)} %get-tuple-element.1071, f32[768]{0:T(1024)S(1)} %get-tuple-element.1068, ...), kind=kOutput, calls=%fused_computation.54.clone.1 | convolution fusion | flops 413859840 | bytes 7825920 | tf_op jit(solution)/shard_map/while/body/eval_jaxpr/dot_general | solution.py:156
  236.2 1.5 fusion.139
  237.7 3.2 fusion.140
  242.2 5.0 %fusion.141 = f32[768,128]{1,0:T(8,128)} fusion(f32[1024,768]{1,0:T(8,128)S(1)} %fusion.139, f32[1024,768]{1,0:T(8,128)} %fusion.140, bf16[768,128]{1,0:T(8,128)(2,1)} %get-tuple-element.1070, f32[768]{0:T(1024)} %get-tuple-element.1072, f32[768]{0:T(1024)} %get-tuple-element.1071, f32[768]{0:T(1024)S(1)} %get-tuple-element.1068, ...), kind=kOutput, calls=%fused_computation.54.clone.1 | convolution fusion | flops 413859840 | bytes 7825920 | tf_op jit(solution)/shard_map/while/body/eval_jaxpr/dot_general | solution.py:156
  247.2 1.0 multiply_convert_fusion
  248.4 10.1 %convolution_bitcast_fusion = f32[8192,512]{1,0:T(8,128)} fusion(bf16[192,8192]{1,0:T(8,128)(2,1)} %all-gather.2.cloned.1.call-done, bf16[24,8,4,128]{3,2,1,0:T(4,128)(2,1)S(1)} %bitcast.121), kind=kOutput, calls=%fused_computation.74 | convolution fusion | flops 1610612736 | bytes 20119552 | tf_op jit(solution)/shard_map/dot_general | solution.py:176
  258.5 95.2 %reduce-scatter.2.cloned.1.call-done = f32[512,512]{1,0:T(8,128)} async-done(((f32[8192,512]{1,0:T(8,128)}), f32[512,512]{1,0:T(8,128)}) %reduce-scatter.2.cloned.1.call-update) | async-done | bytes 1048592 | tf_op jit(solution)/shard_map/reduce_scatter | solution.py:175
  353.7 2.7 dynamic-slice_multiply_fusion
  (83 shorter events, 11.4 us)
Async XLA Ops:
  6.5 99.1 %copy-start = (bf16[8192,128]{1,0:T(8,128)(2,1)S(1)}, bf16[8192,128]{1,0:T(8,128)(2,1)}, u32[]{:S(2)}) copy-start(bf16[8192,128]{1,0:T(8,128)(2,1)} %param.13) | copy-start | bytes 6291460
  6.5 99.1 %all-gather.2.cloned.1.call-start = ((), (), s32[]{:S(2)}) async-start(), calls=%async_computation.1 | async-start | bytes 3342336 | tf_op jit(solution)/shard_map/all_gather | solution.py:51
  7.3 346.5 %reduce-scatter.2.cloned.1.call-start = ((), (), s32[]{:S(2)}) async-start(), calls=%async_computation.2 | async-start | bytes 17825792 | tf_op jit(solution)/shard_map/reduce_scatter | solution.py:175
  18.9 20.0 %copy-start.3 = (bf16[192,512]{1,0:T(8,128)(2,1)S(1)}, bf16[192,512]{1,0:T(8,128)(2,1)}, u32[]{:S(2)}) copy-start(bf16[192,512]{1,0:T(8,128)(2,1)} %param.15) | copy-start | bytes 589828
  105.7 3.1 copy-start.2
  105.7 10.9 %slice-start = ((s8[8388608]{0:T(1024)(128)(4,1)}), s8[4194304]{0:T(1024)(128)(4,1)S(1)}, s32[]{:S(2)}) async-start(s8[8388608]{0:T(1024)(128)(4,1)} %bitcast.126), calls=%async_computation.3 | async-start | bytes 8388608
  108.7 7.9 %slice-start.1 = ((s8[8388608]{0:T(1024)(128)(4,1)}), s8[4194304]{0:T(1024)(128)(4,1)S(1)}, s32[]{:S(2)}) async-start(s8[8388608]{0:T(1024)(128)(4,1)} %bitcast.126), calls=%async_computation.4 | async-start | bytes 8388608
  108.7 9.8 %collective-permute-start = (bf16[192,128]{1,0:T(8,128)(2,1)S(1)}, bf16[192,128]{1,0:T(8,128)(2,1)S(1)}, u32[]{:S(2)}, u32[]{:S(2)}) collective-permute-start(bf16[192,128]{1,0:T(8,128)(2,1)S(1)} %convolution_convert_fusion.1), channel_id=1, source_target_pairs={{0,1},{1,0},{2,3},{3,2},{4,5},{5,4},{6,7},{7,6},{8,9},{9,8},{10,11... | collective-permute-start | bytes 147464 | tf_op jit(solution)/shard_map/ppermute | solution.py:14
  150.3 2.2 copy-start.4
  152.5 0.6 copy-start.5
  156.9 2.2 copy-start.4
  159.1 0.6 copy-start.5
  163.5 2.2 copy-start.4
  165.7 0.6 copy-start.5
  258.5 97.9 %copy-start.1 = (bf16[8192,128]{1,0:T(8,128)(2,1)S(1)}, bf16[8192,128]{1,0:T(8,128)(2,1)}, u32[]{:S(2)}) copy-start(bf16[8192,128]{1,0:T(8,128)(2,1)} %param.13) | copy-start | bytes 6291460
Sparse Core Ops, SparseCore 0:
  9.8 95.7 all-gather.1
  258.6 95.0 reduce-scatter.1
where the time goes:
time: 365 us; the launch traced here: 363 us
  waiting for transfers between devices  150 us (41%)
  matrix products  86.8 us (24%)
  blocking collectives  47.1 us (13%)
  local copies, waits for them, and re-layouts  39.3 us (11%)
  other arithmetic  26.3 us (7%)
  between operations  13.6 us (4%)
    reduce_scatter x1, waiting for transfers between devices, local(): lax.psum_scatter(lax.dot_general(full_tokens, update_local, (((0,), (0,))...  95.2 us
    all_gather x1, waiting for transfers between devices, local(): full_tokens = lax.all_gather(tokens, 'head', axis=1, tiled=True)  53.9 us
    all_gather x2, blocking collectives, gathered(): return lax.all_gather(part, axis, axis=dim, tiled=True)  47.1 us
    shift_right_arithmetic x4, local copies, waits for them, and re-layouts, decode_rows(): bits = packed[:, None, :] >> shifts[None, :, None] & 1  31.5 us
    dot_general x9, matrix products, scores(): jnp.einsum('rd,kd->rk', query_rows, key_piece, preferred_element_type=jnp...  21.8 us
    dot_general x3, matrix products, third_step(): jnp.dot(score_tangent.astype(jnp.bfloat16), key_piece, preferred_element_...  15 us
    convert_element_type x1, other arithmetic, decode_rows(): return (2 * bits - 1).astype(jnp.float32)  12.1 us
    dot_general x6, matrix products, scores(): jnp.einsum('rd,kd->rk', tangent_rows, key_piece, preferred_element_type=j...  10.9 us
  transfers between devices with their start and end apart: 3, of which 2 were waited for; matrix products, arithmetic and copies ran while one was open for 15% of the time, Pallas kernels for 0%

commit v1 on v0

v1 whole, which is shorter than its diff:
```python
import functools

import jax
import jax.numpy as jnp
from jax import lax
from jax.experimental import pallas as pl
from jax.experimental.pallas import tpu as pltpu
from jax.sharding import PartitionSpec as P

MESH = pl.DeviceIdType.MESH
BF16 = jnp.bfloat16
F32 = jnp.float32
BITS = 18
HEAD = 128
CHUNK = 256
LOG2E = 1.4426950408889634
PEERS = ((0, 2), (1, 0), (0, 1), (1, 2), (0, 3), (1, 1), (1, 3))


def mm(a, b):
    return jnp.dot(a, b, preferred_element_type=F32)


def mm_bt(a, b):
    return lax.dot_general(a, b, (((1,), (1,)), ((), ())), preferred_element_type=F32)


def mm_at(a, b):
    return lax.dot_general(a, b, (((0,), (0,)), ((), ())), preferred_element_type=F32)


def kernel(
    tokens_hbm, weight_hbm, kv_weight_hbm, signs_hbm, cot_hbm, out_hbm,
    tok, weight, kv_weight, words, bitmask, sign, cot, acc_q, acc_t, acc_kv,
    col, kv_own, kv_part, kv, qrows, trows, crows, buf_l, buf_t, stat, upd, out,
    load_sem, w_sem, ring_s, ring_r, xh_sem, col_s, col_r, colf_s, colf_r,
    kvx_sem, kv_s, kv_f, kv_r, upd_s, upd_f, upd_r, out_sem,
):
    rows, cols = tokens_hbm.shape
    half, quarter = rows // 2, rows // 4
    s = lax.axis_index("seq")
    h = lax.axis_index("head")
    xl, y, c = s // 8, (s // 2) % 4, s % 2
    xh, z = h // 8, h % 8
    parity = z % 2
    other_core = s + 1 - 2 * c

    def zdev(step):
        return (s, xh * 8 + (z + 8 + step) % 8)

    def rcopy(src, dst, send, recv, dev):
        return pltpu.make_async_remote_copy(
            src_ref=src, dst_ref=dst, send_sem=send, recv_sem=recv, device_id=dev, device_id_type=MESH
        )

    def seq_rows(index, count=rows, shift=0):
        return pl.ds(pl.multiple_of(index * rows + shift, 16), count)

    def feat_rows(f):
        return pl.ds(pl.multiple_of(f * cols, 512), cols)

    def block_of(a, zz):
        return ((xh + a) % 2) * 8 + (zz + 16) % 8

    def w_load(f):
        return pltpu.make_async_copy(weight_hbm.at[feat_rows(f)], weight.at[feat_rows(f)], w_sem.at[f])

    tok_load = pltpu.make_async_copy(tokens_hbm, tok.at[h], load_sem.at[0])
    words_load = pltpu.make_async_copy(signs_hbm, words, load_sem.at[1])
    kvw_load = pltpu.make_async_copy(kv_weight_hbm, kv_weight, load_sem.at[2])
    cot_load = pltpu.make_async_copy(cot_hbm, cot, load_sem.at[3])
    tok_load.start()
    words_load.start()
    w_load(h).start()
    kvw_load.start()

    @pl.loop(1, 16)
    def _(i):
        w_load((h + i) % 16).start()

    cot_load.start()

    barrier = pltpu.get_barrier_semaphore()
    xh_dev = (s, ((xh + 1) % 2) * 8 + z)
    for dev in (zdev(1), zdev(-1), xh_dev):
        pl.semaphore_signal(barrier, inc=1, device_id=dev, device_id_type=MESH)

    @pl.loop(1, 16)
    def _(i):
        pl.semaphore_signal(barrier, inc=1, device_id=((s + i) % 16, h), device_id_type=MESH)

    pl.semaphore_wait(barrier, 18)

    def ring_copy(d, k, a, full=True):
        f = block_of(a, z - (1 - 2 * d) * (k - 1))
        part = tok.at[f] if full else tok.at[f, pl.ds(pl.multiple_of(d * half, 16), half)]
        return rcopy(part, part, ring_s.at[d, k - 1, a], ring_r.at[d, k - 1, a], zdev(1 - 2 * d))

    def ring_arrival(d, k, a, full=True):
        f = block_of(a, z - (1 - 2 * d) * k)
        part = tok.at[f] if full else tok.at[f, pl.ds(pl.multiple_of(d * half, 16), half)]
        return rcopy(part, part, ring_s.at[d, k - 1, a], ring_r.at[d, k - 1, a], zdev(1 - 2 * d))

    def col_copy(f):
        return rcopy(
            tok.at[f, pl.ds(pl.multiple_of(parity * half, 16), half)],
            col.at[seq_rows(s, half, parity * half)],
            col_s.at[f], col_r.at[s], (f, h),
        )

    def col_arrival(src):
        place = col.at[seq_rows(src, half, parity * half)]
        return rcopy(place, place, col_s.at[src], col_r.at[src], (src, h))

    col_local = pltpu.make_async_copy(tok.at[s], col.at[seq_rows(s)], load_sem.at[4])

    def col_send(f):
        @pl.when(f != s)
        def _():
            col_copy(f).start()

        @pl.when(f == s)
        def _():
            col_local.start()

    def project(f):
        w_load(f).wait()
        block = tok[f]
        acc_q[...] += mm(block, weight[feat_rows(f), :])
        acc_t[...] += mm(block, sign[feat_rows(f), :])
        acc_kv[...] += mm(block, kv_weight[feat_rows(f), :])

    tok_load.wait()
    xh_copy = rcopy(tok.at[h], tok.at[h], xh_sem.at[0], xh_sem.at[1], xh_dev)
    xh_copy.start()
    ring_copy(0, 1, 0).start()
    ring_copy(1, 1, 0).start()
    col_send(h)

    acc_q[...] = jnp.zeros_like(acc_q)
    acc_t[...] = jnp.zeros_like(acc_t)
    acc_kv[...] = jnp.zeros_like(acc_kv)
    words_load.wait()
    sub = lax.broadcasted_iota(jnp.int32, (8, HEAD), 0)
    for k in range(BITS):
        shift = sub + (8 * k) % BITS
        shift = jnp.where(shift >= BITS, shift - BITS, shift)
        bitmask[8 * k : 8 * k + 8, :] = jnp.left_shift(jnp.ones_like(shift), shift)

    def decode(g, lo_k, hi_k):
        for lane in range(cols // HEAD):
            w8 = words[pl.ds(pl.multiple_of(g * 8, 8), 8), lane * HEAD : (lane + 1) * HEAD]
            for k2 in range(BITS // 2):
                parts = []
                for k in (2 * k2, 2 * k2 + 1):
                    first, last = 8 * k // BITS, (8 * k + 7) // BITS
                    word = jnp.broadcast_to(w8[first : first + 1], (8, HEAD))
                    if last != first:
                        later = jnp.broadcast_to(w8[last : last + 1], (8, HEAD))
                        word = jnp.where(sub >= BITS * last - 8 * k, later, word)
                    bit = word & bitmask[8 * k : 8 * k + 8, :]
                    parts.append(jnp.where(bit != 0, 1.0, -1.0).astype(F32))
                tile = jnp.concatenate(parts, axis=0).astype(BF16)
                at = pl.multiple_of(g * (8 * BITS) + 16 * k2, 16)
                sign[pl.ds(at, 16), lane * HEAD : (lane + 1) * HEAD] = tile

    groups = words.shape[0] // 8

    @pl.loop(0, groups)
    def _(g):
        decode(g, 0, 0)

    xh_copy.wait_recv()
    ring_copy(0, 1, 1).start()
    ring_copy(1, 1, 1).start()
    col_send(block_of(1, z))
    kvw_load.wait()

    @pl.loop(0, 2)
    def _(a):
        project(block_of(a, z))

    @pl.loop(0, 12)
    def _(m):
        k = m // 4 + 1
        a = (m // 2) % 2
        d = m % 2
        ring_arrival(d, k, a).wait_recv()

        @pl.when(k < 3)
        def _():
            ring_copy(d, k + 1, a).start()

        @pl.when(k == 3)
        def _():
            ring_copy(d, 4, a, full=False).start()

        f = block_of(a, z - (1 - 2 * d) * k)
        col_send(f)
        project(f)

    @pl.loop(0, 2)
    def _(a):
        ring_arrival(0, 4, a, full=False).wait_recv()
        ring_arrival(1, 4, a, full=False).wait_recv()
        f = block_of(a, z + 4)
        col_send(f)
        project(f)

    kv_own[...] = acc_kv[...].astype(BF16)
    kv_dev = (s, h + 1 - 2 * (h % 2))
    kvx = rcopy(kv_own, kv_part, kvx_sem.at[0], kvx_sem.at[1], kv_dev)
    kvx.start()
    cot_load.wait()
    for u in range(2):
        for j in range(2):
            lanes = slice((2 * u + j) * HEAD, (2 * u + j + 1) * HEAD)
            qrows[u, j * rows : (j + 1) * rows, :] = acc_q[:, lanes].astype(BF16)
            trows[u, j * rows : (j + 1) * rows, :] = acc_t[:, lanes].astype(BF16)
            crows[u, j * rows : (j + 1) * rows, :] = cot[:, lanes]
    kvx.wait_recv()
    odd = h % 2 == 1
    mine, theirs = kv_own[...].astype(F32), kv_part[...].astype(F32)
    lower = jnp.where(odd, theirs, mine)
    upper = jnp.where(odd, mine, theirs)
    hw = HEAD // 2
    kv[seq_rows(s), :] = jnp.concatenate(
        [lower[:, :hw], upper[:, :hw], lower[:, hw:], upper[:, hw:]], axis=1
    ).astype(BF16)

    def peer(offset):
        return ((xl + offset[0]) % 2) * 8 + ((y + offset[1]) % 4) * 2 + c

    def gather_copies(place, send, fwd, recv):
        def to(src, dev, sem):
            return rcopy(place(src), place(src), sem, recv.at[src], (dev, h))

        direct = [to(s, peer(o), send.at[i]) for i, o in enumerate(PEERS)]
        passed = [to(s, other_core, fwd.at[7])]
        passed += [to(peer(o), other_core, fwd.at[i]) for i, o in enumerate(PEERS)]
        return to, direct, passed

    def gather_start(parts):
        _, direct, passed = parts
        for copy in direct:
            copy.start()
        passed[0].start()

    def gather_pass(parts, send):
        to, _, passed = parts
        for i, o in enumerate(PEERS):
            to(peer(o), peer(o), send.at[i]).wait_recv()
            passed[i + 1].start()

    def gather_finish(parts, send):
        to, _, _ = parts
        to(other_core, other_core, send.at[0]).wait_recv()
        for i, o in enumerate(PEERS):
            to(peer(o) + 1 - 2 * c, other_core, send.at[i]).wait_recv()

    def gather_drain(parts):
        _, direct, passed = parts
        for copy in direct + passed:
            copy.wait_send()

    kv_parts = gather_copies(lambda i: kv.at[seq_rows(i)], kv_s, kv_f, kv_r)
    gather_start(kv_parts)
    gather_pass(kv_parts, kv_s)

    def colf_copy(d, src):
        place = col.at[seq_rows(src, quarter, parity * half + d * quarter)]
        return rcopy(place, place, colf_s.at[d, src], colf_r.at[d, src], zdev(1 - 2 * d))

    def colf_arrival(d, src):
        place = col.at[seq_rows(src, quarter, (1 - parity) * half + d * quarter)]
        return rcopy(place, place, colf_s.at[d, src], colf_r.at[d, src], zdev(1 - 2 * d))

    @pl.loop(1, 16)
    def _(i):
        src = (s + i) % 16
        col_arrival(src).wait_recv()
        colf_copy(0, src).start()
        colf_copy(1, src).start()

    gather_finish(kv_parts, kv_s)

    scale = HEAD ** (-0.5)
    n_rows = 2 * rows

    def attend(u, b):
        count = (rows * (b + 1) + CHUNK - 1) // CHUNK

        def keys(j):
            return kv[pl.ds(pl.multiple_of(j * CHUNK, CHUNK), CHUNK), :HEAD]

        def values(j):
            return kv[pl.ds(pl.multiple_of(j * CHUNK, CHUNK), CHUNK), HEAD:]

        stat[0] = jnp.full((n_rows, HEAD), -1e30, F32)

        @pl.loop(0, count)
        def _(j):
            key = keys(j)
            rel = lax.broadcasted_iota(jnp.int32, (rows, CHUNK), 1) - lax.broadcasted_iota(
                jnp.int32, (rows, CHUNK), 0
            )
            seen = rel <= b * rows - j * CHUNK
            logits = mm_bt(qrows[u], key)
            buf_t[j] = mm_bt(trows[u], key)
            for p in range(2):
                part = jnp.where(seen, logits[p * rows : (p + 1) * rows], -1e30)
                buf_l[j, p * rows : (p + 1) * rows, :] = part
                high = jnp.maximum(part[:, :HEAD], part[:, HEAD:])
                stat[0, p * rows : (p + 1) * rows, :] = jnp.maximum(
                    stat[0, p * rows : (p + 1) * rows, :], high
                )

        top = jnp.max(stat[0], axis=1, keepdims=True)
        stat[0] = jnp.broadcast_to(top, (n_rows, HEAD))
        stat[1] = jnp.zeros((n_rows, HEAD), F32)
        stat[2] = jnp.zeros((n_rows, HEAD), F32)

        @pl.loop(0, count)
        def _(j):
            for p in range(4):
                r = slice(p * half, (p + 1) * half)
                top = stat[0, r, :]
                total, centre = stat[1, r, :], stat[2, r, :]
                for q in range(2):
                    lanes = slice(q * HEAD, (q + 1) * HEAD)
                    e = jnp.exp2((buf_l[j, r, lanes] - top) * (scale * LOG2E))
                    buf_l[j, r, lanes] = e
                    total += e
                    centre += e * buf_t[j, r, lanes]
                stat[1, r, :] = total
                stat[2, r, :] = centre

        inverse = 1.0 / jnp.sum(stat[1], axis=1, keepdims=True)
        middle = jnp.sum(stat[2], axis=1, keepdims=True) * inverse
        stat[0] = jnp.broadcast_to(inverse, (n_rows, HEAD))
        stat[1] = jnp.broadcast_to(middle, (n_rows, HEAD))
        stat[2] = jnp.zeros((n_rows, HEAD), F32)
        stat[3] = jnp.zeros((n_rows, HEAD), F32)

        @pl.loop(0, count)
        def _(j):
            value = values(j)
            for p in range(2):
                r = slice(p * rows, (p + 1) * rows)
                inverse, middle = stat[0, r, :], stat[1, r, :]
                probs, tangents = [], []
                for q in range(2):
                    lanes = slice(q * HEAD, (q + 1) * HEAD)
                    prob = buf_l[j, r, lanes] * inverse
                    tangent = prob * ((buf_t[j, r, lanes] - middle) * scale)
                    buf_l[j, r, lanes] = prob
                    buf_t[j, r, lanes] = tangent
                    probs.append(prob.astype(BF16))
                    tangents.append(tangent.astype(BF16))
                stat[2, r, :] += mm(jnp.concatenate(probs, axis=1), value)
                stat[3, r, :] += mm(jnp.concatenate(tangents, axis=1), value)

        cot_rows = crows[u].astype(F32)
        delta = jnp.sum(cot_rows * stat[2], axis=1, keepdims=True)
        delta_t = jnp.sum(cot_rows * stat[3], axis=1, keepdims=True)
        stat[0] = jnp.broadcast_to(delta, (n_rows, HEAD))
        stat[1] = jnp.broadcast_to(delta_t, (n_rows, HEAD))
        stat[2] = jnp.zeros((n_rows, HEAD), F32)

        @pl.loop(0, count)
        def _(j):
            key, value = keys(j), values(j)
            for p in range(2):
                r = slice(p * rows, (p + 1) * rows)
                delta, delta_t = stat[0, r, :], stat[1, r, :]
                back = mm_bt(crows[u, r, :], value)
                scores = []
                for q in range(2):
                    lanes = slice(q * HEAD, (q + 1) * HEAD)
                    score = buf_t[j, r, lanes] * (back[:, lanes] - delta) - buf_l[j, r, lanes] * delta_t
                    scores.append(score.astype(BF16))
                stat[2, r, :] += mm(jnp.concatenate(scores, axis=1), key)

        update = (stat[2] * scale).astype(BF16)
        upd[u, seq_rows(b), :] = jnp.concatenate([update[:rows], update[rows:]], axis=1)

    upd_parts = []
    for u in range(2):
        attend(u, s)
        parts = gather_copies(lambda i, u=u: upd.at[u, seq_rows(i)], upd_s.at[u], upd_f.at[u], upd_r.at[u])
        gather_start(parts)
        upd_parts.append(parts)

    @pl.loop(1, 16)
    def _(i):
        src = (s + i) % 16
        colf_arrival(0, src).wait_recv()
        colf_arrival(1, src).wait_recv()

    col_local.wait()
    width = 2 * HEAD
    stores = []
    for u in range(2):
        gather_pass(upd_parts[u], upd_s.at[u])
    for u in range(2):
        gather_finish(upd_parts[u], upd_s.at[u])
        for t in range(2):
            r = slice(t * width, (t + 1) * width)
            hessian = mm_at(col[:, r], upd[u])
            own = sign[pl.ds(pl.multiple_of(s * cols + t * width, 256), width), u * width : (u + 1) * width]
            out[u, r, :] = hessian * own.astype(F32)
        store = pltpu.make_async_copy(
            out.at[u], out_hbm.at[:, pl.ds(u * width, width)], out_sem.at[u]
        )
        store.start()
        stores.append(store)

    for parts in [kv_parts] + upd_parts:
        gather_drain(parts)
    kvx.wait_send()
    xh_copy.wait_send()

    @pl.loop(0, 2)
    def _(d):
        @pl.loop(0, 2)
        def _(a):
            @pl.loop(1, 4)
            def _(k):
                ring_copy(d, k, a).wait_send()

            ring_copy(d, 4, a, full=False).wait_send()

    @pl.loop(1, 16)
    def _(i):
        other = (s + i) % 16
        col_copy(other).wait_send()
        colf_copy(0, other).wait_send()
        colf_copy(1, other).wait_send()

    for store in stores:
        store.wait()


def local(tokens, query_weight, kv_weight, signs, cotangent):
    rows, cols = tokens.shape
    width = query_weight.shape[0]
    words = signs.shape[0]
    total = 16 * rows
    chunks = total // CHUNK
    dma = pltpu.SemaphoreType.DMA
    vmem = pltpu.VMEM
    scratch = [
        vmem((16, rows, cols), BF16),
        vmem((width, cols), BF16),
        vmem((width, HEAD), BF16),
        vmem((words, cols), jnp.int32),
        vmem((8 * BITS, HEAD), jnp.int32),
        vmem((words * BITS, cols), BF16),
        vmem((rows, cols), BF16),
        vmem((rows, cols), F32),
        vmem((rows, cols), F32),
        vmem((rows, HEAD), F32),
        vmem((total, cols), BF16),
        vmem((rows, HEAD), BF16),
        vmem((rows, HEAD), BF16),
        vmem((total, 2 * HEAD), BF16),
        vmem((2, 2 * rows, HEAD), BF16),
        vmem((2, 2 * rows, HEAD), BF16),
        vmem((2, 2 * rows, HEAD), BF16),
        vmem((chunks, 2 * rows, CHUNK), F32),
        vmem((chunks, 2 * rows, CHUNK), F32),
        vmem((4, 2 * rows, HEAD), F32),
        vmem((2, total, 2 * HEAD), BF16),
        vmem((2, cols, 2 * HEAD), F32),
        dma((5,)),
        dma((16,)),
        dma((2, 4, 2)),
        dma((2, 4, 2)),
        dma((2,)),
        dma((16,)),
        dma((16,)),
        dma((2, 16)),
        dma((2, 16)),
        dma((2,)),
        dma((7,)),
        dma((8,)),
        dma((16,)),
        dma((2, 7)),
        dma((2, 8)),
        dma((2, 16)),
        dma((2,)),
    ]
    return pl.pallas_call(
        kernel,
        out_shape=jax.ShapeDtypeStruct((width // 16, cols), F32),
        in_specs=[pl.BlockSpec(memory_space=pl.ANY)] * 5,
        out_specs=pl.BlockSpec(memory_space=pl.ANY),
        scratch_shapes=scratch,
        compiler_params=pltpu.CompilerParams(
            collective_id=0, has_side_effects=True, vmem_limit_bytes=60 * 1024 * 1024
        ),
        name="salience",
    )(tokens, query_weight, kv_weight, signs, cotangent)


def solution(mesh):
    placed = (P("seq", "head"), P(None, "head"), P(None, "head"), P(None, "head"), P("seq", "head"))
    return jax.shard_map(
        local, mesh=mesh, in_specs=placed, out_specs=P("seq", "head"), check_vma=False
    )
```

time: 365 us -> 111 us (0.30)
  waiting for transfers between devices: 150 us -> 0 us
  Pallas kernels: 0 us -> 108 us
  matrix products: 86.8 us -> 0 us
  blocking collectives: 47.1 us -> 0 us
  local copies, waits for them, and re-layouts: 39.3 us -> 2.26 us
  other arithmetic: 26.3 us -> 0 us
  between operations: 13.6 us -> 0.01 us
    pallas_call x0 -> x1, Pallas kernels: none -> 108 us  [local(): pl.pallas_call(kernel, out_shape=jax.ShapeDtypeStruct((width // 16, cols)...]
    reduce_scatter x1 -> x0, waiting for transfers between devices: 95.2 us -> none  [local(): lax.psum_scatter(lax.dot_general(full_tokens, update_local, (((0,), (0,))...]
    dot_general x28 -> x0, matrix products: 86.8 us -> none  [the longest x9 21.8 us: scores(): jnp.einsum('rd,kd->rk', query_rows, key_piece, preferred_element_type=jnp...]
    all_gather x1 -> x0, waiting for transfers between devices: 53.9 us -> none  [local(): full_tokens = lax.all_gather(tokens, 'head', axis=1, tiled=True)]
    all_gather x2 -> x0, blocking collectives: 47.1 us -> none  [gathered(): return lax.all_gather(part, axis, axis=dim, tiled=True)]
    shift_right_arithmetic x4 -> x0, local copies, waits for them, and re-layouts: 31.5 us -> none  [decode_rows(): bits = packed[:, None, :] >> shifts[None, :, None] & 1]
    convert_element_type x2 -> x0, other arithmetic: 13.2 us -> none  [the longest x1 12.1 us: decode_rows(): return (2 * bits - 1).astype(jnp.float32)]
    reduce_sum x4 -> x0, other arithmetic: 4.77 us -> none  [the longest x3 2.68 us: first_step(): jnp.sum(weights_exp, axis=1)]
  transfers between devices with their start and end apart: 3 -> 0, of which waited for: 2 -> 0; matrix products, arithmetic and copies ran while one was open for 15% -> 0% of each run, Pallas kernels for 0% -> 0%
where the time goes in v1:
time: 111 us; the launch traced here: 110 us
  Pallas kernels  108 us (97%)
  local copies, waits for them, and re-layouts  2.26 us (2%)
    pallas_call x1, Pallas kernels, local(): pl.pallas_call(kernel, out_shape=jax.ShapeDtypeStruct((width // 16, cols)...  108 us
    unnamed x1, local copies, waits for them, and re-layouts  2.26 us

profile of v1, /device:TPU:1, one launch (start us, length us, event | category | flops | bytes accessed | tf_op | source)
XLA Modules:
  0.0 109.8 jit_solution(3127641846520559362)
XLA Ops:
  0.0 107.5 %salience.1 = f32[512,512]{1,0:T(8,128)} custom-call(bf16[192,512]{1,0:T(8,128)(2,1)} %tokens_hbm.1, bf16[8192,512]{1,0:T(8,128)(2,1)} %weight_hbm.1, bf16[8192,128]{1,0:T(8,128)(2,1)} %kv_weight_hbm.1, s32[456,512]{1,0:T(8,128)} %signs_hbm.1, bf16[192,512]{1,0:T(8,128)(2,1)} %cot_hbm.1), custom_call_target="tpu_custom_call" | custom-call | tf_op jit(solution)/shard_map/salience/pallas_call | solution.py:493
  107.6 2.3 %copy.7 = f32[512,512]{1,0:T(8,128)} copy(f32[512,512]{1,0:T(8,128)} %salience.1) | data formatting | bytes 2097152

commit v2 on v1

v2 whole, which is shorter than its diff:
```python
import functools

import jax
import jax.numpy as jnp
from jax import lax
from jax.experimental import pallas as pl
from jax.experimental.pallas import tpu as pltpu
from jax.sharding import PartitionSpec as P

MESH = pl.DeviceIdType.MESH
BF16 = jnp.bfloat16
F32 = jnp.float32
BITS = 18
HEAD = 128
CHUNK = 384
LOG2E = 1.4426950408889634


def mm(a, b):
    return jnp.dot(a, b, preferred_element_type=F32)


def mm_bt(a, b):
    return lax.dot_general(a, b, (((1,), (1,)), ((), ())), preferred_element_type=F32)


def mm_at(a, b):
    return lax.dot_general(a, b, (((0,), (0,)), ((), ())), preferred_element_type=F32)


def kernel(
    tokens_hbm, weight_hbm, kv_weight_hbm, signs_hbm, cot_hbm, out_hbm,
    tok, weight, kv_weight, words, bitmask, sign, cot, acc_q, acc_t, acc_kv,
    col, kv_own, kv_part, kv, qrows, trows, crows, buf_l, buf_t, buf_b, scores, stat, upd, out,
    load_sem, w_sem, ring_s, ring_r, xh_s, xh_r, col_s, col_r, colf_s, colf_r,
    swap_s, swap_r, kvx_sem, kv_s, kv_f, kv_r, upd_s, upd_f, upd_r, out_sem,
):
    rows, cols = tokens_hbm.shape
    half, quarter = rows // 2, rows // 4
    s = lax.axis_index("seq")
    h = lax.axis_index("head")
    xl, y, c = s // 8, (s // 2) % 4, s % 2
    xh, z = h // 8, h % 8
    parity = z % 2
    other_core = s + 1 - 2 * c

    def zdev(step):
        return (s, xh * 8 + (z + 8 + step) % 8)

    def rcopy(src, dst, send, recv, dev):
        return pltpu.make_async_remote_copy(
            src_ref=src, dst_ref=dst, send_sem=send, recv_sem=recv, device_id=dev, device_id_type=MESH
        )

    pair = 15 - s

    def part_rows(part):
        return pl.ds(pl.multiple_of(part * half, 16), half)

    def place_rows(src, part, count=half, shift=0):
        unit = (part + src // 8) % 2
        return pl.ds(pl.multiple_of((unit * 16 + src) * half + shift, 16), count)

    def feat_rows(f):
        return pl.ds(pl.multiple_of(f * cols, 512), cols)

    def block_of(a, zz):
        return ((xh + a) % 2) * 8 + (zz + 16) % 8

    def w_load(f):
        return pltpu.make_async_copy(weight_hbm.at[feat_rows(f)], weight.at[feat_rows(f)], w_sem.at[f])

    tok_load = pltpu.make_async_copy(tokens_hbm.at[part_rows(0)], tok.at[h, part_rows(0)], load_sem.at[0])
    words_load = pltpu.make_async_copy(signs_hbm, words, load_sem.at[1])
    kvw_load = pltpu.make_async_copy(kv_weight_hbm, kv_weight, load_sem.at[2])
    cot_load = pltpu.make_async_copy(cot_hbm.at[part_rows(0)], cot.at[part_rows(0)], load_sem.at[3])
    tok_load.start()
    words_load.start()
    w_load(h).start()
    kvw_load.start()

    @pl.loop(1, 16)
    def _(i):
        w_load((h + i) % 16).start()

    cot_load.start()

    barrier = pltpu.get_barrier_semaphore()
    xh_dev = (s, ((xh + 1) % 2) * 8 + z)
    for dev in (zdev(1), zdev(-1), xh_dev):
        pl.semaphore_signal(barrier, inc=1, device_id=dev, device_id_type=MESH)

    @pl.loop(1, 16)
    def _(i):
        pl.semaphore_signal(barrier, inc=1, device_id=((s + i) % 16, h), device_id_type=MESH)

    pl.semaphore_wait(barrier, 18)

    def chunk(f, part):
        return tok.at[f, part_rows(part)]

    def ring_copy(d, k, a, part):
        ref = chunk(block_of(a, z - (1 - 2 * d) * (k - 1)), part)
        return rcopy(
            ref, ref, ring_s.at[d, k - 1, a, part], ring_r.at[d, k - 1, a, part], zdev(1 - 2 * d)
        )

    def ring_arrival(d, k, a, part):
        ref = chunk(block_of(a, z - (1 - 2 * d) * k), part)
        return rcopy(
            ref, ref, ring_s.at[d, k - 1, a, part], ring_r.at[d, k - 1, a, part], zdev(1 - 2 * d)
        )

    def xh_copy(part):
        return rcopy(chunk(h, part), chunk(h, part), xh_s.at[part], xh_r.at[part], xh_dev)

    def xh_arrival(part):
        ref = chunk(block_of(1, z), part)
        return rcopy(ref, ref, xh_s.at[part], xh_r.at[part], xh_dev)

    def col_copy(f):
        return rcopy(
            chunk(f, parity),
            col.at[place_rows(s, parity)],
            col_s.at[f], col_r.at[s], (f, h),
        )

    def col_arrival(src):
        place = col.at[place_rows(src, parity)]
        return rcopy(place, place, col_s.at[src], col_r.at[src], (src, h))

    def col_local(part):
        return pltpu.make_async_copy(
            chunk(s, part), col.at[place_rows(s, part)], load_sem.at[4 + part]
        )

    def col_send(f):
        @pl.when(f != s)
        def _():
            col_copy(f).start()

    def col_keep(f):
        @pl.when(f == s)
        def _():
            col_local(0).start()
            col_local(1).start()

    tok_swap = rcopy(
        tokens_hbm.at[part_rows(1)], tok.at[h, part_rows(1)], swap_s.at[0], swap_r.at[0], (pair, h)
    )
    cot_swap = rcopy(
        cot_hbm.at[part_rows(1)], cot.at[part_rows(1)], swap_s.at[1], swap_r.at[1], (pair, h)
    )
    tok_swap.start()
    tok_load.wait()

    def own_send(part):
        xh_copy(part).start()
        ring_copy(0, 1, 0, part).start()
        ring_copy(1, 1, 0, part).start()

        @pl.when(part == parity)
        def _():
            col_send(h)

    own_send(0)
    acc_q[...] = jnp.zeros_like(acc_q)
    acc_t[...] = jnp.zeros_like(acc_t)
    acc_kv[...] = jnp.zeros_like(acc_kv)
    words_load.wait()
    sub = lax.broadcasted_iota(jnp.int32, (8, HEAD), 0)
    for k in range(BITS):
        shift = sub + (8 * k) % BITS
        shift = jnp.where(shift >= BITS, shift - BITS, shift)
        bitmask[8 * k : 8 * k + 8, :] = jnp.left_shift(jnp.ones_like(shift), shift)

    def decode_group(g):
        for lane in range(cols // HEAD):
            w8 = words[pl.ds(pl.multiple_of(g * 8, 8), 8), lane * HEAD : (lane + 1) * HEAD]
            for k2 in range(BITS // 2):
                parts = []
                for k in (2 * k2, 2 * k2 + 1):
                    first, last = 8 * k // BITS, (8 * k + 7) // BITS
                    word = jnp.broadcast_to(w8[first : first + 1], (8, HEAD))
                    if last != first:
                        later = jnp.broadcast_to(w8[last : last + 1], (8, HEAD))
                        word = jnp.where(sub >= BITS * last - 8 * k, later, word)
                    bit = word & bitmask[8 * k : 8 * k + 8, :]
                    parts.append(jnp.where(bit != 0, 1.0, -1.0).astype(F32))
                tile = jnp.concatenate(parts, axis=0).astype(BF16)
                at = pl.multiple_of(g * (8 * BITS) + 16 * k2, 16)
                sign[pl.ds(at, 16), lane * HEAD : (lane + 1) * HEAD] = tile

    def decode(f):
        low = f * cols // (8 * BITS)
        high = (f * cols + cols - 1) // (8 * BITS)

        @pl.loop(low, high + 1)
        def _(g):
            decode_group(g)

    def project_kv(f):
        acc_kv[...] += mm(tok[f], kv_weight[feat_rows(f), :])

    def project_q(f):
        w_load(f).wait()
        block = tok[f]
        acc_q[...] += mm(block, weight[feat_rows(f), :])
        acc_t[...] += mm(block, sign[feat_rows(f), :])

    def other_send(part):
        xh_arrival(part).wait_recv()
        ring_copy(0, 1, 1, part).start()
        ring_copy(1, 1, 1, part).start()

    other_send(0)
    tok_swap.wait_recv()
    own_send(1)
    col_keep(h)
    decode(h)
    other_send(1)
    cot_swap.start()
    col_send(block_of(1, z))
    col_keep(block_of(1, z))
    kvw_load.wait()
    project_kv(h)
    project_q(h)

    @pl.loop(0, 24)
    def _(m):
        k = m // 8 + 1
        a = (m // 4) % 2
        part = (m // 2) % 2
        d = m % 2
        ring_arrival(d, k, a, part).wait_recv()

        @pl.when((k < 3) | (part == d))
        def _():
            ring_copy(d, k + 1, a, part).start()

        f = block_of(a, z - (1 - 2 * d) * k)

        @pl.when(part == parity)
        def _():
            col_send(f)

        @pl.when(part == 0)
        def _():
            decode(f)

        @pl.when(part == 1)
        def _():
            col_keep(f)
            project_kv(f)
            project_q(f)

        @pl.when(m == 1)
        def _():
            decode(block_of(1, z))
            project_kv(block_of(1, z))
            project_q(block_of(1, z))

    decode(block_of(0, z + 4))
    decode(block_of(1, z + 4))

    @pl.loop(0, 2)
    def _(a):
        f = block_of(a, z + 4)
        ring_arrival(0, 4, a, 0).wait_recv()
        ring_arrival(1, 4, a, 1).wait_recv()
        project_kv(f)

    def colf_copy(d, src):
        place = col.at[place_rows(src, parity, quarter, d * quarter)]
        return rcopy(place, place, colf_s.at[d, src], colf_r.at[d, src], zdev(1 - 2 * d))

    def colf_arrival(d, src):
        place = col.at[place_rows(src, 1 - parity, quarter, d * quarter)]
        return rcopy(place, place, colf_s.at[d, src], colf_r.at[d, src], zdev(1 - 2 * d))

    away = (z + 8 - s % 8) % 8
    far = (away >= 3) & (away <= 5)

    def col_forward(when):
        @pl.when(when)
        def _():
            @pl.loop(1, 16)
            def _(i):
                src = (s + i) % 16
                col_arrival(src).wait_recv()
                colf_copy(0, src).start()
                colf_copy(1, src).start()

    kv_own[...] = acc_kv[...].astype(BF16)
    kv_dev = (s, h + 1 - 2 * (h % 2))
    kvx = rcopy(kv_own, kv_part, kvx_sem.at[0], kvx_sem.at[1], kv_dev)
    kvx.start()

    @pl.loop(0, 2)
    def _(a):
        project_q(block_of(a, z + 4))

    cot_load.wait()
    cot_swap.wait_recv()
    heads = cols // HEAD
    for u in range(2):
        at = pl.ds(pl.multiple_of((u + xl) % 2 * half, 16), half)
        for j in range(heads):
            lanes = slice(j * HEAD, (j + 1) * HEAD)
            into = slice(j * half, (j + 1) * half)
            qrows[u, into, :] = acc_q[at, lanes].astype(BF16)
            trows[u, into, :] = acc_t[at, lanes].astype(BF16)
            crows[u, into, :] = cot[at, lanes]
    kvx.wait_recv()
    odd = h % 2 == 1
    mine, theirs = kv_own[...].astype(F32), kv_part[...].astype(F32)
    lower = jnp.where(odd, theirs, mine)
    upper = jnp.where(odd, mine, theirs)
    hw = HEAD // 2
    kv[s] = jnp.concatenate(
        [lower[:, :hw], upper[:, :hw], lower[:, hw:], upper[:, hw:]], axis=1
    ).astype(BF16)

    x_peer = (xl + 1) % 2 * 8 + y * 2 + c

    def y_peer(step):
        return xl * 8 + (y + step) % 4 * 2 + c

    def xy_peer(step):
        return (xl + 1) % 2 * 8 + (y + step) % 4 * 2 + c

    class Gather:
        def __init__(self, place, send, fwd, recv):
            self.place, self.send, self.fwd, self.recv = place, send, fwd, recv

        def to(self, src, dev, sem):
            return rcopy(self.place(src), self.place(src), sem, self.recv.at[src], (dev, h))

        def arrived(self, src):
            self.to(src, x_peer, self.send.at[0]).wait_recv()

        def share(self, src):
            self.to(src, other_core, self.fwd.at[src // 2]).start()

        def start(self):
            self.to(s, x_peer, self.send.at[0]).start()
            for step in (2, 1, 3):
                self.to(s, y_peer(step), self.send.at[step]).start()
            self.share(s)

        def middle(self):
            @pl.when(c == 0)
            def _():
                self.arrived(x_peer)
                for i, step in enumerate((2, 1, 3)):
                    self.to(x_peer, y_peer(step), self.send.at[4 + i]).start()
                self.share(x_peer)

            @pl.when(c == 1)
            def _():
                for i, step in enumerate((1, 3, 2)):
                    self.arrived(y_peer(step))
                    self.to(y_peer(step), x_peer, self.send.at[4 + i]).start()
                    self.share(y_peer(step))

        def end(self):
            @pl.when(c == 0)
            def _():
                for step in (1, 3, 2):
                    self.arrived(y_peer(step))
                    self.share(y_peer(step))

            @pl.when(c == 1)
            def _():
                self.arrived(x_peer)
                self.share(x_peer)

            for step in (1, 3, 2):
                self.arrived(xy_peer(step))
                self.share(xy_peer(step))

        def finish(self):
            for step in range(4):
                self.arrived(y_peer(step) + 1 - 2 * c)
                self.arrived(xy_peer(step) + 1 - 2 * c)

        def drain(self):
            for i in range(7):
                self.to(s, x_peer, self.send.at[i]).wait_send()
            for i in range(8):
                self.to(s, other_core, self.fwd.at[i]).wait_send()

    kv_gather = Gather(lambda src: kv.at[src], kv_s, kv_f, kv_r)
    kv_gather.start()

    @pl.loop(0, 2)
    def _(a):
        col_send(block_of(a, z + 4))
        col_keep(block_of(a, z + 4))

    kv_gather.middle()
    col_forward(jnp.logical_not(far))
    kv_gather.end()
    col_forward(far)
    kv_gather.finish()

    scale = HEAD ** (-0.5)
    n_rows = heads * half
    pieces = CHUNK // half
    tiles = CHUNK // HEAD

    def attend(u, b, hook):
        count = (b + pieces) // pieces

        def load(j, lanes):
            parts = []
            for i in range(pieces // 2):
                owner = j * (pieces // 2) + i
                parts += [kv[owner, :half, lanes], kv[15 - owner, half:, lanes]]
            return jnp.concatenate(parts, axis=0)

        key_lanes, value_lanes = slice(0, HEAD), slice(HEAD, 2 * HEAD)
        runs = [slice(p * half, (p + 1) * half) for p in range(heads)]
        strips = [slice(q * HEAD, (q + 1) * HEAD) for q in range(tiles)]

        def logits_of(j, last):
            buf_l[j] = mm_bt(qrows[u], load(j, key_lanes))
            if last:
                rel = lax.broadcasted_iota(jnp.int32, (half, CHUNK), 1) - lax.broadcasted_iota(
                    jnp.int32, (half, CHUNK), 0
                )
                seen = rel <= b * half - j * CHUNK
            for r in runs:
                if last:
                    buf_l[j, r, :] = jnp.where(seen, buf_l[j, r, :], -1e30)
                high = stat[0, r, :]
                for lanes in strips:
                    high = jnp.maximum(high, buf_l[j, r, lanes])
                stat[0, r, :] = high

        stat[0] = jnp.full((n_rows, HEAD), -1e30, F32)

        @pl.loop(0, count - 1)
        def _(j):
            logits_of(j, False)

        logits_of(count - 1, True)
        stat[0] = jnp.broadcast_to(jnp.max(stat[0], axis=1, keepdims=True), (n_rows, HEAD))
        for i in range(1, 5):
            stat[i] = jnp.zeros((n_rows, HEAD), F32)

        @pl.loop(0, count)
        def _(j):
            buf_t[j] = mm_bt(trows[u], load(j, key_lanes))
            buf_b[j] = mm_bt(crows[u], load(j, value_lanes))
            for r in runs:
                top = stat[0, r, :]
                sums = [stat[i, r, :] for i in range(1, 5)]
                for lanes in strips:
                    e = jnp.exp2((buf_l[j, r, lanes] - top) * (scale * LOG2E))
                    buf_l[j, r, lanes] = e
                    back = buf_b[j, r, lanes]
                    et = e * buf_t[j, r, lanes]
                    for i, term in enumerate((e, et, e * back, et * back)):
                        sums[i] += term
                for i in range(4):
                    stat[i + 1, r, :] = sums[i]

        hook()
        sums = [jnp.sum(stat[i], axis=1, keepdims=True) for i in range(1, 5)]
        inverse = 1.0 / sums[0]
        middle = sums[1] * inverse
        delta = sums[2] * inverse
        delta_t = sums[3] * inverse - middle * delta
        for i, value in enumerate((middle, delta, delta_t)):
            stat[i] = jnp.broadcast_to(value, (n_rows, HEAD))
        stat[3] = jnp.zeros((n_rows, HEAD), F32)

        @pl.loop(0, count)
        def _(j):
            for r in runs:
                middle, delta, delta_t = stat[0, r, :], stat[1, r, :], stat[2, r, :]
                for lanes in strips:
                    score = buf_l[j, r, lanes] * (
                        (buf_t[j, r, lanes] - middle) * (buf_b[j, r, lanes] - delta) - delta_t
                    )
                    scores[r, lanes] = score.astype(BF16)
            stat[3] += mm(scores[...], load(j, key_lanes))

        update = (stat[3] * (inverse * (scale * scale))).astype(BF16)
        upd[upd_rows(u, s), :] = jnp.concatenate(
            [update[p * half : (p + 1) * half] for p in range(heads)], axis=1
        )

    def upd_rows(u, src):
        return pl.ds(pl.multiple_of((u * 16 + src) * half, 16), half)

    early = jnp.minimum(2 * s, 31 - 2 * s)
    gathers = [
        Gather(lambda src, u=u: upd.at[upd_rows(u, src)], upd_s.at[u], upd_f.at[u], upd_r.at[u])
        for u in range(2)
    ]
    attend(0, early, lambda: None)
    gathers[0].start()
    attend(1, 31 - early, gathers[0].middle)
    gathers[1].start()
    gathers[0].end()
    gathers[1].middle()
    gathers[0].finish()

    @pl.loop(1, 16)
    def _(i):
        src = (s + i) % 16
        colf_arrival(0, src).wait_recv()
        colf_arrival(1, src).wait_recv()

    col_local(0).wait()
    col_local(1).wait()
    side = 16 * half

    def hessian(u, t):
        run = slice(u * side, (u + 1) * side)
        return mm_at(col[run, t * 256 : (t + 1) * 256], upd[run, :])

    for t in range(cols // 256):
        out[t * 256 : (t + 1) * 256, :] = hessian(0, t)
    gathers[1].end()
    gathers[1].finish()
    stores = []
    for t in range(cols // 256):
        r = slice(t * 256, (t + 1) * 256)
        own = sign[pl.ds(pl.multiple_of(s * cols + t * 256, 256), 256), :]
        out[r, :] = (out[r, :] + hessian(1, t)) * own.astype(F32)
        store = pltpu.make_async_copy(out.at[r], out_hbm.at[r], out_sem.at[t])
        store.start()
        stores.append(store)

    for gather in [kv_gather] + gathers:
        gather.drain()
    tok_swap.wait_send()
    cot_swap.wait_send()
    kvx.wait_send()
    for part in range(2):
        xh_copy(part).wait_send()

    @pl.loop(0, 2)
    def _(d):
        @pl.loop(0, 2)
        def _(a):
            @pl.loop(1, 4)
            def _(k):
                ring_copy(d, k, a, 0).wait_send()
                ring_copy(d, k, a, 1).wait_send()

            ring_copy(d, 4, a, d).wait_send()

    @pl.loop(1, 16)
    def _(i):
        other = (s + i) % 16
        col_copy(other).wait_send()
        colf_copy(0, other).wait_send()
        colf_copy(1, other).wait_send()

    for store in stores:
        store.wait()


def local(tokens, query_weight, kv_weight, signs, cotangent):
    rows, cols = tokens.shape
    width = query_weight.shape[0]
    words = signs.shape[0]
    total = 16 * rows
    chunks = total // CHUNK
    dma = pltpu.SemaphoreType.DMA
    vmem = pltpu.VMEM
    scratch = [
        vmem((16, rows, cols), BF16),
        vmem((width, cols), BF16),
        vmem((width, HEAD), BF16),
        vmem((words, cols), jnp.int32),
        vmem((8 * BITS, HEAD), jnp.int32),
        vmem((words * BITS, cols), BF16),
        vmem((rows, cols), BF16),
        vmem((rows, cols), F32),
        vmem((rows, cols), F32),
        vmem((rows, HEAD), F32),
        vmem((total, cols), BF16),
        vmem((rows, HEAD), BF16),
        vmem((rows, HEAD), BF16),
        vmem((16, rows, 2 * HEAD), BF16),
        vmem((2, 2 * rows, HEAD), BF16),
        vmem((2, 2 * rows, HEAD), BF16),
        vmem((2, 2 * rows, HEAD), BF16),
        vmem((chunks, 2 * rows, CHUNK), F32),
        vmem((chunks, 2 * rows, CHUNK), F32),
        vmem((chunks, 2 * rows, CHUNK), F32),
        vmem((2 * rows, CHUNK), BF16),
        vmem((5, 2 * rows, HEAD), F32),
        vmem((total, cols), BF16),
        vmem((cols, cols), F32),
        dma((6,)),
        dma((16,)),
        dma((2, 4, 2, 2)),
        dma((2, 4, 2, 2)),
        dma((2,)),
        dma((2,)),
        dma((16,)),
        dma((16,)),
        dma((2, 16)),
        dma((2, 16)),
        dma((2,)),
        dma((2,)),
        dma((2,)),
        dma((7,)),
        dma((8,)),
        dma((16,)),
        dma((2, 7)),
        dma((2, 8)),
        dma((2, 16)),
        dma((2,)),
    ]
    return pl.pallas_call(
        kernel,
        out_shape=jax.ShapeDtypeStruct((width // 16, cols), F32),
        in_specs=[pl.BlockSpec(memory_space=pl.ANY)] * 5,
        out_specs=pl.BlockSpec(memory_space=pl.ANY),
        scratch_shapes=scratch,
        compiler_params=pltpu.CompilerParams(
            collective_id=0, has_side_effects=True, vmem_limit_bytes=60 * 1024 * 1024
        ),
        name="salience",
    )(tokens, query_weight, kv_weight, signs, cotangent)


def solution(mesh):
    placed = (P("seq", "head"), P(None, "head"), P(None, "head"), P(None, "head"), P("seq", "head"))
    return jax.shard_map(
        local, mesh=mesh, in_specs=placed, out_specs=P("seq", "head"), check_vma=False
    )
```

time: 111 us -> 95.7 us (0.86)
  the two profiles are of different devices: /device:TPU:1 before, /device:TPU:90 now
where the time goes in v2:
time: 95.7 us; the launch traced here: 95.5 us
  Pallas kernels  93.3 us (97%)
  local copies, waits for them, and re-layouts  2.26 us (2%)
    pallas_call x1, Pallas kernels, local(): pl.pallas_call(kernel, out_shape=jax.ShapeDtypeStruct((width // 16, cols)...  93.3 us
    unnamed x1, local copies, waits for them, and re-layouts  2.26 us

profile of v2, /device:TPU:90, one launch (start us, length us, event | category | flops | bytes accessed | tf_op | source)
XLA Modules:
  0.0 95.5 jit_solution(9884316560069535016)
XLA Ops:
  0.0 93.3 %salience.1 = f32[512,512]{1,0:T(8,128)} custom-call(bf16[192,512]{1,0:T(8,128)(2,1)} %tokens_hbm.1, bf16[8192,512]{1,0:T(8,128)(2,1)} %weight_hbm.1, bf16[8192,128]{1,0:T(8,128)(2,1)} %kv_weight_hbm.1, s32[456,512]{1,0:T(8,128)} %signs_hbm.1, bf16[192,512]{1,0:T(8,128)(2,1)} %cot_hbm.1), custom_call_target="tpu_custom_call" | custom-call | tf_op jit(solution)/shard_map/salience/pallas_call | solution.py:622
  93.3 2.3 %copy.7 = f32[512,512]{1,0:T(8,128)} copy(f32[512,512]{1,0:T(8,128)} %salience.1) | data formatting | bytes 2097152

commit v3 on v2

--- a/solution.py
+++ b/solution.py
@@ -29,11 +29,11 @@
 
 
 def kernel(
-    tokens_hbm, weight_hbm, kv_weight_hbm, signs_hbm, cot_hbm, out_hbm,
+    tokens_hbm, weight_hbm, kv_weight_hbm, signs_hbm, cot_hbm, out,
     tok, weight, kv_weight, words, bitmask, sign, cot, acc_q, acc_t, acc_kv,
-    col, kv_own, kv_part, kv, qrows, trows, crows, buf_l, buf_t, buf_b, scores, stat, upd, out,
+    col, kv, whole, qrows, trows, crows, buf_l, buf_t, buf_b, scores, stat, acc_u, upd,
     load_sem, w_sem, ring_s, ring_r, xh_s, xh_r, col_s, col_r, colf_s, colf_r,
-    swap_s, swap_r, kvx_sem, kv_s, kv_f, kv_r, upd_s, upd_f, upd_r, out_sem,
+    swap_s, swap_r, kvx_sem, kv_s, kv_f, kv_r, upd_s, upd_f, upd_r,
 ):
     rows, cols = tokens_hbm.shape
     half, quarter = rows // 2, rows // 4
@@ -67,6 +67,15 @@
     def block_of(a, zz):
         return ((xh + a) % 2) * 8 + (zz + 16) % 8
 
+    barrier = pltpu.get_barrier_semaphore()
+    xh_dev = (s, ((xh + 1) % 2) * 8 + z)
+    for dev in (zdev(1), zdev(-1), xh_dev):
+        pl.semaphore_signal(barrier, inc=1, device_id=dev, device_id_type=MESH)
+
+    @pl.loop(1, 16)
+    def _(i):
+        pl.semaphore_signal(barrier, inc=1, device_id=((s + i) % 16, h), device_id_type=MESH)
+
     def w_load(f):
         return pltpu.make_async_copy(weight_hbm.at[feat_rows(f)], weight.at[feat_rows(f)], w_sem.at[f])
 
@@ -84,15 +93,6 @@
         w_load((h + i) % 16).start()
 
     cot_load.start()
-
-    barrier = pltpu.get_barrier_semaphore()
-    xh_dev = (s, ((xh + 1) % 2) * 8 + z)
-    for dev in (zdev(1), zdev(-1), xh_dev):
-        pl.semaphore_signal(barrier, inc=1, device_id=dev, device_id_type=MESH)
-
-    @pl.loop(1, 16)
-    def _(i):
-        pl.semaphore_signal(barrier, inc=1, device_id=((s + i) % 16, h), device_id_type=MESH)
 
     pl.semaphore_wait(barrier, 18)
 
@@ -229,8 +229,8 @@
     @pl.loop(0, 24)
     def _(m):
         k = m // 8 + 1
-        a = (m // 4) % 2
-        part = (m // 2) % 2
+        part = (m // 4) % 2
+        a = (m // 2) % 2
         d = m % 2
         ring_arrival(d, k, a, part).wait_recv()
 
@@ -291,19 +291,118 @@
                 colf_copy(0, src).start()
                 colf_copy(1, src).start()
 
-    kv_own[...] = acc_kv[...].astype(BF16)
-    kv_dev = (s, h + 1 - 2 * (h % 2))
-    kvx = rcopy(kv_own, kv_part, kvx_sem.at[0], kvx_sem.at[1], kv_dev)
+    x_peer = (xl + 1) % 2 * 8 + y * 2 + c
+
+    def y_peer(step):
+        return xl * 8 + (y + step) % 4 * 2 + c
+
+    def xy_peer(step):
+        return (xl + 1) % 2 * 8 + (y + step) % 4 * 2 + c
+
+    class Gather:
+        def __init__(self, place, send, fwd, recv):
+            self.place, self.send, self.fwd, self.recv = place, send, fwd, recv
+
+        def to(self, src, dev, i, p):
+            ref = self.place(src, p)
+            return rcopy(ref, ref, self.send.at[i, p], self.recv.at[src, p], (dev, h))
+
+        def arrived(self, src, p):
+            self.to(src, x_peer, 0, p).wait_recv()
+
+        def share(self, src, p):
+            ref = self.place(src, p)
+            rcopy(ref, ref, self.fwd.at[src // 2, p], self.recv.at[src, p], (other_core, h)).start()
+
+        def start(self, pieces=(0, 1)):
+            def along_x():
+                for p in pieces:
+                    self.to(s, x_peer, 0, p).start()
+
+            def along_y():
+                for p in pieces:
+                    for step in (1, 3, 2):
+                        self.to(s, y_peer(step), step, p).start()
+                    self.share(s, p)
+
+            @pl.when(c == 0)
+            def _():
+                along_x()
+                along_y()
+
+            @pl.when(c == 1)
+            def _():
+                along_y()
+                along_x()
+
+        def middle(self, p):
+            @pl.when(c == 0)
+            def _():
+                self.arrived(x_peer, p)
+                for i, step in enumerate((1, 3, 2)):
+                    self.to(x_peer, y_peer(step), 4 + i, p).start()
+                self.share(x_peer, p)
+
+            @pl.when(c == 1)
+            def _():
+                for i, step in enumerate((1, 3, 2)):
+                    self.arrived(y_peer(step), p)
+                    self.to(y_peer(step), x_peer, 4 + i, p).start()
+                    self.share(y_peer(step), p)
+
+        def end(self, p):
+            @pl.when(c == 0)
+            def _():
+                for step in (1, 3, 2):
+                    self.arrived(y_peer(step), p)
+                    self.share(y_peer(step), p)
+
+            @pl.when(c == 1)
+            def _():
+                self.arrived(x_peer, p)
+                self.share(x_peer, p)
+
+            for step in (1, 3, 2):
+                self.arrived(xy_peer(step), p)
+                self.share(xy_peer(step), p)
+
+        def finish(self, p):
+            for step in range(4):
+                self.arrived(y_peer(step) + 1 - 2 * c, p)
+                self.arrived(xy_peer(step) + 1 - 2 * c, p)
+
+        def drain(self):
+            for p in range(2):
+                for i in range(7):
+                    self.to(s, x_peer, i, p).wait_send()
+                ref = self.place(s, p)
+                for i in range(8):
+                    rcopy(ref, ref, self.fwd.at[i, p], self.recv.at[s, p], (other_core, h)).wait_send()
+
+    odd = h % 2
+    kv[odd, s] = acc_kv[...].astype(BF16)
+    kvx = rcopy(
+        kv.at[odd, s], kv.at[odd, s], kvx_sem.at[0], kvx_sem.at[1], (s, h + 1 - 2 * odd)
+    )
+    kvx_arrival = rcopy(
+        kv.at[1 - odd, s], kv.at[1 - odd, s], kvx_sem.at[0], kvx_sem.at[1], (s, h + 1 - 2 * odd)
+    )
+    kv_gather = Gather(lambda src, p: kv.at[(odd + p) % 2, src], kv_s, kv_f, kv_r)
     kvx.start()
+    kv_gather.start((0,))
 
     @pl.loop(0, 2)
     def _(a):
         project_q(block_of(a, z + 4))
 
+    kvx_arrival.wait_recv()
+    kv_gather.start((1,))
+    kv_gather.middle(0)
+
     cot_load.wait()
     cot_swap.wait_recv()
     heads = cols // HEAD
-    for u in range(2):
+    def fill_rows(u):
         at = pl.ds(pl.multiple_of((u + xl) % 2 * half, 16), half)
         for j in range(heads):
             lanes = slice(j * HEAD, (j + 1) * HEAD)
@@ -311,120 +410,56 @@
             qrows[u, into, :] = acc_q[at, lanes].astype(BF16)
             trows[u, into, :] = acc_t[at, lanes].astype(BF16)
             crows[u, into, :] = cot[at, lanes]
-    kvx.wait_recv()
-    odd = h % 2 == 1
-    mine, theirs = kv_own[...].astype(F32), kv_part[...].astype(F32)
-    lower = jnp.where(odd, theirs, mine)
-    upper = jnp.where(odd, mine, theirs)
-    hw = HEAD // 2
-    kv[s] = jnp.concatenate(
-        [lower[:, :hw], upper[:, :hw], lower[:, hw:], upper[:, hw:]], axis=1
-    ).astype(BF16)
-
-    x_peer = (xl + 1) % 2 * 8 + y * 2 + c
-
-    def y_peer(step):
-        return xl * 8 + (y + step) % 4 * 2 + c
-
-    def xy_peer(step):
-        return (xl + 1) % 2 * 8 + (y + step) % 4 * 2 + c
-
-    class Gather:
-        def __init__(self, place, send, fwd, recv):
-            self.place, self.send, self.fwd, self.recv = place, send, fwd, recv
-
-        def to(self, src, dev, sem):
-            return rcopy(self.place(src), self.place(src), sem, self.recv.at[src], (dev, h))
-
-        def arrived(self, src):
-            self.to(src, x_peer, self.send.at[0]).wait_recv()
-
-        def share(self, src):
-            self.to(src, other_core, self.fwd.at[src // 2]).start()
-
-        def start(self):
-            self.to(s, x_peer, self.send.at[0]).start()
-            for step in (2, 1, 3):
-                self.to(s, y_peer(step), self.send.at[step]).start()
-            self.share(s)
-
-        def middle(self):
-            @pl.when(c == 0)
-            def _():
-                self.arrived(x_peer)
-                for i, step in enumerate((2, 1, 3)):
-                    self.to(x_peer, y_peer(step), self.send.at[4 + i]).start()
-                self.share(x_peer)
-
-            @pl.when(c == 1)
-            def _():
-                for i, step in enumerate((1, 3, 2)):
-                    self.arrived(y_peer(step))
-                    self.to(y_peer(step), x_peer, self.send.at[4 + i]).start()
-                    self.share(y_peer(step))
-
-        def end(self):
-            @pl.when(c == 0)
-            def _():
-                for step in (1, 3, 2):
-                    self.arrived(y_peer(step))
-                    self.share(y_peer(step))
-
-            @pl.when(c == 1)
-            def _():
-                self.arrived(x_peer)
-                self.share(x_peer)
-
-            for step in (1, 3, 2):
-                self.arrived(xy_peer(step))
-                self.share(xy_peer(step))
-
-        def finish(self):
-            for step in range(4):
-                self.arrived(y_peer(step) + 1 - 2 * c)
-                self.arrived(xy_peer(step) + 1 - 2 * c)
-
-        def drain(self):
-            for i in range(7):
-                self.to(s, x_peer, self.send.at[i]).wait_send()
-            for i in range(8):
-                self.to(s, other_core, self.fwd.at[i]).wait_send()
-
-    kv_gather = Gather(lambda src: kv.at[src], kv_s, kv_f, kv_r)
-    kv_gather.start()
+
+    fill_rows(0)
+    kv_gather.middle(1)
+    kv_gather.end(0)
 
     @pl.loop(0, 2)
     def _(a):
         col_send(block_of(a, z + 4))
         col_keep(block_of(a, z + 4))
 
-    kv_gather.middle()
+    fill_rows(1)
+    kv_gather.end(1)
     col_forward(jnp.logical_not(far))
-    kv_gather.end()
+    kv_gather.finish(0)
+    kv_gather.finish(1)
     col_forward(far)
-    kv_gather.finish()
+
+    low = lax.broadcasted_iota(jnp.int32, (rows, HEAD), 1) < HEAD // 2
+
+    def turned(block):
+        return jnp.concatenate([block[:, HEAD // 2 :], block[:, : HEAD // 2]], axis=1)
+
+    @pl.loop(0, 16)
+    def _(src):
+        lower, upper = kv[0, src].astype(F32), kv[1, src].astype(F32)
+        whole[0, src] = jnp.where(low, lower, turned(upper)).astype(BF16)
+        whole[1, src] = jnp.where(low, turned(lower), upper).astype(BF16)
 
     scale = HEAD ** (-0.5)
     n_rows = heads * half
     pieces = CHUNK // half
     tiles = CHUNK // HEAD
 
-    def attend(u, b, hook):
+    def attend(u, b, hook_sums, hook_half):
         count = (b + pieces) // pieces
 
-        def load(j, lanes):
+        def load(j, which):
             parts = []
             for i in range(pieces // 2):
                 owner = j * (pieces // 2) + i
-                parts += [kv[owner, :half, lanes], kv[15 - owner, half:, lanes]]
+                for src, at in ((owner, slice(0, half)), (15 - owner, slice(half, rows))):
+                    parts.append(whole[which, src, at])
             return jnp.concatenate(parts, axis=0)
 
-        key_lanes, value_lanes = slice(0, HEAD), slice(HEAD, 2 * HEAD)
+        keys, values = 0, 1
         runs = [slice(p * half, (p + 1) * half) for p in range(heads)]
         strips = [slice(q * HEAD, (q + 1) * HEAD) for q in range(tiles)]
 
         def logits_of(j, last):
-            buf_l[j] = mm_bt(qrows[u], load(j, key_lanes))
+            buf_l[j] = mm_bt(qrows[u], load(j, keys))
             if last:
                 rel = lax.broadcasted_iota(jnp.int32, (half, CHUNK), 1) - lax.broadcasted_iota(
                     jnp.int32, (half, CHUNK), 0
@@ -451,8 +486,8 @@
 
         @pl.loop(0, count)
         def _(j):
-            buf_t[j] = mm_bt(trows[u], load(j, key_lanes))
-            buf_b[j] = mm_bt(crows[u], load(j, value_lanes))
+            buf_t[j] = mm_bt(trows[u], load(j, keys))
+            buf_b[j] = mm_bt(crows[u], load(j, values))
             for r in runs:
                 top = stat[0, r, :]
                 sums = [stat[i, r, :] for i in range(1, 5)]
@@ -466,7 +501,7 @@
                 for i in range(4):
                     stat[i + 1, r, :] = sums[i]
 
-        hook()
+        hook_sums()
         sums = [jnp.sum(stat[i], axis=1, keepdims=True) for i in range(1, 5)]
         inverse = 1.0 / sums[0]
         middle = sums[1] * inverse
@@ -474,39 +509,48 @@
         delta_t = sums[3] * inverse - middle * delta
         for i, value in enumerate((middle, delta, delta_t)):
             stat[i] = jnp.broadcast_to(value, (n_rows, HEAD))
-        stat[3] = jnp.zeros((n_rows, HEAD), F32)
-
-        @pl.loop(0, count)
-        def _(j):
-            for r in runs:
-                middle, delta, delta_t = stat[0, r, :], stat[1, r, :], stat[2, r, :]
-                for lanes in strips:
-                    score = buf_l[j, r, lanes] * (
-                        (buf_t[j, r, lanes] - middle) * (buf_b[j, r, lanes] - delta) - delta_t
-                    )
-                    scores[r, lanes] = score.astype(BF16)
-            stat[3] += mm(scores[...], load(j, key_lanes))
-
-        update = (stat[3] * (inverse * (scale * scale))).astype(BF16)
-        upd[upd_rows(u, s), :] = jnp.concatenate(
-            [update[p * half : (p + 1) * half] for p in range(heads)], axis=1
-        )
+        acc_u[...] = jnp.zeros_like(acc_u)
+
+        factor = inverse * (scale * scale)
+        for p in range(2):
+            both = slice(p * n_rows // 2, (p + 1) * n_rows // 2)
+
+            @pl.loop(0, count)
+            def _(j):
+                for r in runs[2 * p : 2 * p + 2]:
+                    middle, delta, delta_t = stat[0, r, :], stat[1, r, :], stat[2, r, :]
+                    for lanes in strips:
+                        score = buf_l[j, r, lanes] * (
+                            (buf_t[j, r, lanes] - middle) * (buf_b[j, r, lanes] - delta) - delta_t
+                        )
+                        scores[r, lanes] = score.astype(BF16)
+                acc_u[both, :] += mm(scores[both, :], load(j, keys))
+
+            update = (acc_u[both, :] * factor[both]).astype(BF16)
+            upd[p, upd_rows(u, s), :] = jnp.concatenate([update[:half], update[half:]], axis=1)
+            hook_half(p)
 
     def upd_rows(u, src):
         return pl.ds(pl.multiple_of((u * 16 + src) * half, 16), half)
 
     early = jnp.minimum(2 * s, 31 - 2 * s)
     gathers = [
-        Gather(lambda src, u=u: upd.at[upd_rows(u, src)], upd_s.at[u], upd_f.at[u], upd_r.at[u])
+        Gather(lambda src, p, u=u: upd.at[p, upd_rows(u, src)], upd_s.at[u], upd_f.at[u], upd_r.at[u])
         for u in range(2)
     ]
-    attend(0, early, lambda: None)
-    gathers[0].start()
-    attend(1, 31 - early, gathers[0].middle)
-    gathers[1].start()
-    gathers[0].end()
-    gathers[1].middle()
-    gathers[0].finish()
+
+    def first_middle():
+        gathers[0].middle(0)
+        gathers[0].middle(1)
+
+    attend(0, early, lambda: None, lambda p: gathers[0].start((p,)))
+    attend(1, 31 - early, first_middle, lambda p: gathers[1].start((p,)))
+    gathers[0].end(0)
+    gathers[1].middle(0)
+    gathers[0].end(1)
+    gathers[1].middle(1)
+    gathers[0].finish(0)
+    gathers[0].finish(1)
 
     @pl.loop(1, 16)
     def _(i):
@@ -518,22 +562,27 @@
     col_local(1).wait()
     side = 16 * half
 
-    def hessian(u, t):
+    width = cols // 2
+
+    def hessian(u, t, p):
         run = slice(u * side, (u + 1) * side)
-        return mm_at(col[run, t * 256 : (t + 1) * 256], upd[run, :])
-
-    for t in range(cols // 256):
-        out[t * 256 : (t + 1) * 256, :] = hessian(0, t)
-    gathers[1].end()
-    gathers[1].finish()
-    stores = []
-    for t in range(cols // 256):
-        r = slice(t * 256, (t + 1) * 256)
-        own = sign[pl.ds(pl.multiple_of(s * cols + t * 256, 256), 256), :]
-        out[r, :] = (out[r, :] + hessian(1, t)) * own.astype(F32)
-        store = pltpu.make_async_copy(out.at[r], out_hbm.at[r], out_sem.at[t])
-        store.start()
-        stores.append(store)
+        return mm_at(col[run, t * 256 : (t + 1) * 256], upd[p, run, :])
+
+    places = [
+        (t, p, slice(t * 256, (t + 1) * 256), slice(p * width, (p + 1) * width))
+        for p in range(2)
+        for t in range(cols // 256)
+    ]
+    for t, p, r, lanes in places:
+        out[r, lanes] = hessian(0, t, p)
+    for p in range(2):
+        gathers[1].end(p)
+    for p in range(2):
+        gathers[1].finish(p)
+        for t, q, r, lanes in places:
+            if p == q:
+                own = sign[pl.ds(pl.multiple_of(s * cols + t * 256, 256), 256), lanes]
+                out[r, lanes] = (out[r, lanes] + hessian(1, t, p)) * own.astype(F32)
 
     for gather in [kv_gather] + gathers:
         gather.drain()
@@ -560,9 +609,6 @@
         col_copy(other).wait_send()
         colf_copy(0, other).wait_send()
         colf_copy(1, other).wait_send()
-
-    for store in stores:
-        store.wait()
 
 
 def local(tokens, query_weight, kv_weight, signs, cotangent):
@@ -585,9 +631,8 @@
         vmem((rows, cols), F32),
         vmem((rows, HEAD), F32),
         vmem((total, cols), BF16),
-        vmem((rows, HEAD), BF16),
-        vmem((rows, HEAD), BF16),
-        vmem((16, rows, 2 * HEAD), BF16),
+        vmem((2, 16, rows, HEAD), BF16),
+        vmem((2, 16, rows, HEAD), BF16),
         vmem((2, 2 * rows, HEAD), BF16),
         vmem((2, 2 * rows, HEAD), BF16),
         vmem((2, 2 * rows, HEAD), BF16),
@@ -596,8 +641,8 @@
         vmem((chunks, 2 * rows, CHUNK), F32),
         vmem((2 * rows, CHUNK), BF16),
         vmem((5, 2 * rows, HEAD), F32),
-        vmem((total, cols), BF16),
-        vmem((cols, cols), F32),
+        vmem((2 * rows, HEAD), F32),
+        vmem((2, total, cols // 2), BF16),
         dma((6,)),
         dma((16,)),
         dma((2, 4, 2, 2)),
@@ -611,19 +656,18 @@
         dma((2,)),
         dma((2,)),
         dma((2,)),
-        dma((7,)),
-        dma((8,)),
-        dma((16,)),
-        dma((2, 7)),
-        dma((2, 8)),
-        dma((2, 16)),
-        dma((2,)),
+        dma((7, 2)),
+        dma((8, 2)),
+        dma((16, 2)),
+        dma((2, 7, 2)),
+        dma((2, 8, 2)),
+        dma((2, 16, 2)),
     ]
     return pl.pallas_call(
         kernel,
-        out_shape=jax.ShapeDtypeStruct((width // 16, cols), F32),
+        out_shape=pltpu.VMEM((width // 16, cols), F32),
         in_specs=[pl.BlockSpec(memory_space=pl.ANY)] * 5,
-        out_specs=pl.BlockSpec(memory_space=pl.ANY),
+        out_specs=pl.BlockSpec(memory_space=pltpu.VMEM),
         scratch_shapes=scratch,
         compiler_params=pltpu.CompilerParams(
             collective_id=0, has_side_effects=True, vmem_limit_bytes=60 * 1024 * 1024

time: 95.7 us -> 92 us (0.961)
  the two profiles are of different devices: /device:TPU:90 before, /device:TPU:1 now
where the time goes in v3:
time: 92 us; the launch traced here: 91.9 us
  Pallas kernels  91 us (99%)
  local copies, waits for them, and re-layouts  0.97 us (1%)
    pallas_call x1, Pallas kernels, local(): pl.pallas_call(kernel, out_shape=pltpu.VMEM((width // 16, cols), F32), in...  91 us

profile of v3, /device:TPU:1, one launch (start us, length us, event | category | flops | bytes accessed | tf_op | source)
XLA Modules:
  0.0 91.9 jit_solution(1947990155465946046)
XLA Ops:
  0.0 91.0 %salience.1 = f32[512,512]{1,0:T(8,128)S(1)} custom-call(bf16[192,512]{1,0:T(8,128)(2,1)} %tokens_hbm.1, bf16[8192,512]{1,0:T(8,128)(2,1)} %weight_hbm.1, bf16[8192,128]{1,0:T(8,128)(2,1)} %kv_weight_hbm.1, s32[456,512]{1,0:T(8,128)} %signs_hbm.1, bf16[192,512]{1,0:T(8,128)(2,1)} %cot_hbm.1), custom_call_target="tpu_custom_call" | custom-call | tf_op jit(solution)/shard_map/salience/pallas_call | solution.py:666
  91.0 1.0 %copy.7 = f32[512,512]{1,0:T(8,128)} copy(f32[512,512]{1,0:T(8,128)S(1)} %salience.1) | data formatting | bytes 2097152

commit v4 on v3

--- a/solution.py
+++ b/solution.py
@@ -12,7 +12,7 @@
 F32 = jnp.float32
 BITS = 18
 HEAD = 128
-CHUNK = 384
+CHUNK = 768
 LOG2E = 1.4426950408889634
 
 
@@ -281,16 +281,6 @@
     away = (z + 8 - s % 8) % 8
     far = (away >= 3) & (away <= 5)
 
-    def col_forward(when):
-        @pl.when(when)
-        def _():
-            @pl.loop(1, 16)
-            def _(i):
-                src = (s + i) % 16
-                col_arrival(src).wait_recv()
-                colf_copy(0, src).start()
-                colf_copy(1, src).start()
-
     x_peer = (xl + 1) % 2 * 8 + y * 2 + c
 
     def y_peer(step):
@@ -378,6 +368,20 @@
                 ref = self.place(s, p)
                 for i in range(8):
                     rcopy(ref, ref, self.fwd.at[i, p], self.recv.at[s, p], (other_core, h)).wait_send()
+
+    def cores(src):
+        return [src, src + 1 - 2 * c]
+
+    close = [other_core] + cores(y_peer(1)) + cores(y_peer(3)) + cores(x_peer)
+    distant = cores(xy_peer(1)) + cores(xy_peer(3)) + cores(y_peer(2)) + cores(xy_peer(2))
+
+    def col_forward(when, sources):
+        @pl.when(when)
+        def _():
+            for src in sources:
+                col_arrival(src).wait_recv()
+                colf_copy(0, src).start()
+                colf_copy(1, src).start()
 
     odd = h % 2
     kv[odd, s] = acc_kv[...].astype(BF16)
@@ -422,10 +426,10 @@
 
     fill_rows(1)
     kv_gather.end(1)
-    col_forward(jnp.logical_not(far))
+    col_forward(jnp.logical_not(far), close + distant)
     kv_gather.finish(0)
     kv_gather.finish(1)
-    col_forward(far)
+    col_forward(far, close)
 
     low = lax.broadcasted_iota(jnp.int32, (rows, HEAD), 1) < HEAD // 2
 
@@ -534,17 +538,27 @@
         return pl.ds(pl.multiple_of((u * 16 + src) * half, 16), half)
 
     early = jnp.minimum(2 * s, 31 - 2 * s)
-    gathers = [
-        Gather(lambda src, p, u=u: upd.at[p, upd_rows(u, src)], upd_s.at[u], upd_f.at[u], upd_r.at[u])
-        for u in range(2)
-    ]
-
-    def first_middle():
-        gathers[0].middle(0)
-        gathers[0].middle(1)
-
-    attend(0, early, lambda: None, lambda p: gathers[0].start((p,)))
-    attend(1, 31 - early, first_middle, lambda p: gathers[1].start((p,)))
+    def update_gather(u):
+        return Gather(
+            lambda src, p: upd.at[p, upd_rows(u, src)], upd_s.at[u], upd_f.at[u], upd_r.at[u]
+        )
+
+    gathers = [update_gather(0), update_gather(1)]
+
+    @pl.loop(0, 2)
+    def _(u):
+        def first_middle():
+            col_forward(far & (u == 0), distant)
+
+            @pl.when(u == 1)
+            def _():
+                gathers[0].middle(0)
+                gathers[0].middle(1)
+
+        attend(
+            u, early + u * (31 - 2 * early), first_middle, lambda p: update_gather(u).start((p,))
+        )
+
     gathers[0].end(0)
     gathers[1].middle(0)
     gathers[0].end(1)

time: 92 us -> 91.5 us (level)
  no operation moved by 1% of the time
where the time goes in v4:
time: 91.5 us; the launch traced here: 91.4 us
  Pallas kernels  90.5 us (99%)
  local copies, waits for them, and re-layouts  0.97 us (1%)
    pallas_call x1, Pallas kernels, local(): pl.pallas_call(kernel, out_shape=pltpu.VMEM((width // 16, cols), F32), in...  90.5 us

profile of v4, /device:TPU:1, one launch (start us, length us, event | category | flops | bytes accessed | tf_op | source)
XLA Modules:
  0.0 91.4 jit_solution(16276319360888269170)
XLA Ops:
  0.0 90.5 %salience.1 = f32[512,512]{1,0:T(8,128)S(1)} custom-call(bf16[192,512]{1,0:T(8,128)(2,1)} %tokens_hbm.1, bf16[8192,512]{1,0:T(8,128)(2,1)} %weight_hbm.1, bf16[8192,128]{1,0:T(8,128)(2,1)} %kv_weight_hbm.1, s32[456,512]{1,0:T(8,128)} %signs_hbm.1, bf16[192,512]{1,0:T(8,128)(2,1)} %cot_hbm.1), custom_call_target="tpu_custom_call" | custom-call | tf_op jit(solution)/shard_map/salience/pallas_call | solution.py:680
  90.5 1.0 %copy.7 = f32[512,512]{1,0:T(8,128)} copy(f32[512,512]{1,0:T(8,128)S(1)} %salience.1) | data formatting | bytes 2097152

commit v5 on v4

--- a/solution.py
+++ b/solution.py
@@ -425,6 +425,24 @@
         col_keep(block_of(a, z + 4))
 
     fill_rows(1)
+
+    tok_swap.wait_send()
+    cot_swap.wait_send()
+    kvx.wait_send()
+    for part in range(2):
+        xh_copy(part).wait_send()
+
+    @pl.loop(0, 2)
+    def _(d):
+        @pl.loop(0, 2)
+        def _(a):
+            @pl.loop(1, 4)
+            def _(k):
+                ring_copy(d, k, a, 0).wait_send()
+                ring_copy(d, k, a, 1).wait_send()
+
+            ring_copy(d, 4, a, d).wait_send()
+
     kv_gather.end(1)
     col_forward(jnp.logical_not(far), close + distant)
     kv_gather.finish(0)
@@ -589,6 +607,17 @@
     ]
     for t, p, r, lanes in places:
         out[r, lanes] = hessian(0, t, p)
+
+    kv_gather.drain()
+    gathers[0].drain()
+
+    @pl.loop(1, 16)
+    def _(i):
+        other = (s + i) % 16
+        col_copy(other).wait_send()
+        colf_copy(0, other).wait_send()
+        colf_copy(1, other).wait_send()
+
     for p in range(2):
         gathers[1].end(p)
     for p in range(2):
@@ -598,31 +627,7 @@
                 own = sign[pl.ds(pl.multiple_of(s * cols + t * 256, 256), 256), lanes]
                 out[r, lanes] = (out[r, lanes] + hessian(1, t, p)) * own.astype(F32)
 
-    for gather in [kv_gather] + gathers:
-        gather.drain()
-    tok_swap.wait_send()
-    cot_swap.wait_send()
-    kvx.wait_send()
-    for part in range(2):
-        xh_copy(part).wait_send()
-
-    @pl.loop(0, 2)
-    def _(d):
-        @pl.loop(0, 2)
-        def _(a):
-            @pl.loop(1, 4)
-            def _(k):
-                ring_copy(d, k, a, 0).wait_send()
-                ring_copy(d, k, a, 1).wait_send()
-
-            ring_copy(d, 4, a, d).wait_send()
-
-    @pl.loop(1, 16)
-    def _(i):
-        other = (s + i) % 16
-        col_copy(other).wait_send()
-        colf_copy(0, other).wait_send()
-        colf_copy(1, other).wait_send()
+    gathers[1].drain()
 
 
 def local(tokens, query_weight, kv_weight, signs, cotangent):

time: 91.5 us -> 91 us (level)
  no operation moved by 1% of the time
where the time goes in v5:
time: 91 us
  Pallas kernels  90 us (99%)
  local copies, waits for them, and re-layouts  0.97 us (1%)
    pallas_call x1, Pallas kernels, local(): pl.pallas_call(kernel, out_shape=pltpu.VMEM((width // 16, cols), F32), in...  90 us

profile of v5, /device:TPU:1, one launch (start us, length us, event | category | flops | bytes accessed | tf_op | source)
XLA Modules:
  0.0 91.0 jit_solution(9828127754910113458)
XLA Ops:
  0.0 90.0 %salience.1 = f32[512,512]{1,0:T(8,128)S(1)} custom-call(bf16[192,512]{1,0:T(8,128)(2,1)} %tokens_hbm.1, bf16[8192,512]{1,0:T(8,128)(2,1)} %weight_hbm.1, bf16[8192,128]{1,0:T(8,128)(2,1)} %kv_weight_hbm.1, s32[456,512]{1,0:T(8,128)} %signs_hbm.1, bf16[192,512]{1,0:T(8,128)(2,1)} %cot_hbm.1), custom_call_target="tpu_custom_call" | custom-call | tf_op jit(solution)/shard_map/salience/pallas_call | solution.py:685
  90.0 1.0 %copy.7 = f32[512,512]{1,0:T(8,128)} copy(f32[512,512]{1,0:T(8,128)S(1)} %salience.1) | data formatting | bytes 2097152
